TPU v7x, 128 devices: a whole 4x4x4 slice. The times are simulated.
128 devices in a mesh: sec: 8 (over x_hi, z), row: 16 (over x_lo, y, core).
Axes of the slice: x: 4 (x_hi: 2, x_lo: 2; x = x_hi * 2 + x_lo), y: 4, z: 4, core: 2. Of those that a mesh axis runs over, the one named last changes fastest.
Arguments:
- raw_sections: bfloat16 [8, 2048, 8192], P('sec', None, 'row'), may hold values from -6 to 6
- shift_rows: int32 [8, 16, 64], P('sec', 'row'), may hold values from -1 to 1
- source_cols: int32 [8, 16, 64], P('sec', 'row'), may hold values from 0 to 63
Outputs:
- vertical_scores: float32 [8, 3, 16, 64, 128], P('sec', None, 'row')
- horizontal_scores: float32 [8, 3, 16, 64, 128], P('sec', None, 'row')
All inputs are finite; a program needn't handle non-finite values.
Results may differ from a plain program's by a relative error of at most 0.0003.
Values may be sent and summed in bfloat16 or wider, within the bound.
No kernel may reach another device: no remote copies, remote signals or barrier semaphores. Data moves between devices by JAX's collectives and lax.ppermute only.
A program may use at most 640 MiB of HBM per device.

v0:
```python
import jax
import jax.numpy as jnp
from jax import lax
from jax.sharding import PartitionSpec as P

BLOCK = 128


def extended(block, sides, width):
    for axis, dim in sides:
        count = lax.axis_size(axis)
        forward = [(i, i + 1) for i in range(count - 1)]
        backward = [(target, source) for source, target in forward]
        low = lax.ppermute(
            lax.slice_in_dim(block, block.shape[dim] - width, None, axis=dim), axis, forward
        )
        high = lax.ppermute(lax.slice_in_dim(block, 0, width, axis=dim), axis, backward)
        block = jnp.concatenate([low, block, high], axis=dim)
    return block


def from_behind(block, axis, distance):
    devices = range(lax.axis_size(axis))
    route = [(i - distance, i) for i in devices if i - distance in devices]
    return lax.ppermute(block, axis, route)


def lag_profile(matrix):
    block_len = matrix.shape[-1]
    leading = matrix.shape[:-2]
    doubled = jnp.concatenate([matrix, matrix], -1)
    flattened = doubled.reshape(leading + (2 * block_len * block_len,))
    stride = 2 * block_len + 1
    upper_part = (
        flattened[..., : (block_len - 1) * stride]
        .reshape(leading + (block_len - 1, stride))[..., :block_len]
        .sum(-2)
    )
    last_row = flattened[..., (block_len - 1) * stride : (block_len - 1) * stride + block_len]
    return upper_part + last_row


def pair_scores(current, current_energy, previous):
    row_corr = jnp.einsum("bpjq,bsjq->bjps", current, previous, preferred_element_type=jnp.float32)
    col_corr = jnp.einsum("bpjq,bpjt->bjqt", current, previous, preferred_element_type=jnp.float32)
    previous_energy = jnp.einsum(
        "bpjq,bpjq->bj", previous, previous, preferred_element_type=jnp.float32
    ) / (BLOCK * BLOCK)
    scaling = 1.0 / (BLOCK * jnp.sqrt(current_energy * previous_energy + 1e-06))
    return (lag_profile(row_corr) * scaling[..., None], lag_profile(col_corr) * scaling[..., None])


def body(raw_sections, shift_rows, source_cols):
    column = raw_sections[0]
    stripe = lax.all_to_all(column, "row", split_axis=0, concat_axis=1, tiled=True)
    padded = extended(stripe, (("row", 0),), BLOCK)
    block_rows = padded.shape[0] // BLOCK - 2
    block_cols = padded.shape[1] // BLOCK
    source_blocks = padded.reshape(block_rows + 2, BLOCK, block_cols, BLOCK)
    sources = jnp.stack(
        [
            source_blocks[0:block_rows],
            source_blocks[1 : block_rows + 1],
            source_blocks[2 : block_rows + 2],
        ],
        1,
    )
    shifts = shift_rows[0]
    columns = source_cols[0]
    row_pick = shifts[:, None, :] == (jnp.arange(3, dtype=jnp.int32) - 1)[None, :, None]
    col_pick = columns[:, None, :] == jnp.arange(block_cols, dtype=jnp.int32)[None, :, None]
    onehot = (row_pick[:, :, None, :] & col_pick[:, None, :, :]).astype(jnp.bfloat16)
    warped = jnp.einsum(
        "brcj,brpcq->bpjq", onehot, sources, preferred_element_type=jnp.float32
    ).astype(jnp.bfloat16)
    current_energy = jnp.einsum(
        "bpjq,bpjq->bj", warped, warped, preferred_element_type=jnp.float32
    ) / (BLOCK * BLOCK)
    others = []
    for offset in (1, 2, 3):
        others.append(from_behind(warped, "sec", offset))
    vertical_list = []
    horizontal_list = []
    for previous in others:
        vertical, horizontal = pair_scores(warped, current_energy, previous)
        vertical_list.append(vertical)
        horizontal_list.append(horizontal)
    vertical_all = jnp.stack(vertical_list)
    horizontal_all = jnp.stack(horizontal_list)
    return (vertical_all[None], horizontal_all[None])


def solution(mesh):
    return jax.shard_map(
        body,
        mesh=mesh,
        in_specs=(P("sec", None, "row"), P("sec", "row", None), P("sec", "row", None)),
        out_specs=(P("sec", None, "row", None, None), P("sec", None, "row", None, None)),
        check_vma=False,
    )
```

profile of v0, /device:TPU:84, one launch (start us, length us, event | category | flops | bytes accessed | tf_op | source)
XLA Modules:
  0.0 606.3 jit_solution(7373321221064297056)
XLA Ops:
  0.6 29.4 %all_to_all.19 = bf16[16,128,512]{2,1,0:T(8,128)(2,1)S(1)} all-to-all(bf16[16,128,512]{2,1,0:T(8,128)(2,1)} %bitcast.125), channel_id=1, replica_groups=mesh['sec'=8,'row'=16] {'row'}, dimensions={0} | all-to-all | bytes 4194304 | tf_op jit(solution)/shard_map/all_to_all | solution.py:55
  40.8 4.4 stack.37
  45.1 15.0 %collective-permute-done = bf16[128,8192]{0,1:T(8,128)(2,1)} collective-permute-done((bf16[128,8192]{0,1:T(8,128)(2,1)}, bf16[128,8192]{0,1:T(8,128)(2,1)}, u32[]{:S(2)}, u32[]{:S(2)}) %collective-permute-start) | collective-permute-done | bytes 2097184 | tf_op jit(solution)/shard_map/ppermute | solution.py:14
  60.1 4.1 copy.107
  64.3 4.2 copy.109
  68.4 5.0 fusion.8
  80.0 88.3 %collective-permute-done.2 = bf16[1,128,64,128]{3,2,1,0:T(8,128)(2,1)S(1)} collective-permute-done((bf16[1,128,64,128]{3,2,1,0:T(8,128)(2,1)S(1)}, bf16[1,128,64,128]{3,2,1,0:T(8,128)(2,1)S(1)}, u32[]{:S(2)}, u32[]{:S(2)}) %collective-permute-start.2) | collective-permute-done | bytes 2097184 | tf_op jit(solution)/shard_map/ppermute | solution.py:25
  169.7 4.2 copy.76
  173.9 4.2 copy.79
  178.1 6.1 %convolution_bitcast_fusion.5 = f32[1,64,128,128]{2,3,1,0:T(8,128)} fusion(bf16[128,64,128]{0,2,1:T(8,128)(2,1)} %copy.76, bf16[128,64,128]{2,1,0:T(8,128)(2,1)S(1)} %bitcast.117), kind=kOutput, calls=%fused_computation.32 | convolution fusion | flops 268435456 | bytes 8388608 | tf_op jit(solution)/shard_map/bpjq,bsjq->bjps/dot_general | solution.py:44
  184.1 4.4 convolution_bitcast_fusion.4
  188.5 4.3 convolution_bitcast_fusion.2
  192.8 4.4 convolution_bitcast_fusion.1
  197.2 99.9 %collective-permute-done.4 = bf16[1,128,64,128]{3,2,1,0:T(8,128)(2,1)} collective-permute-done((bf16[1,128,64,128]{3,2,1,0:T(8,128)(2,1)S(1)}, bf16[1,128,64,128]{3,2,1,0:T(8,128)(2,1)}, u32[]{:S(2)}, u32[]{:S(2)}) %collective-permute-start.4) | collective-permute-done | bytes 2097184 | tf_op jit(solution)/shard_map/ppermute | solution.py:25
  297.1 4.3 copy.82
  301.4 6.1 convolution_bitcast_fusion.3
  307.5 4.3 convolution_bitcast_fusion
  311.8 3.8 pad_maximum_fusion
  315.6 9.0 %copy.68 = f32[1,64,128,256]{3,2,1,0:T(8,128)} copy(f32[1,64,128,256]{2,3,1,0:T(8,128)} %pad_maximum_fusion) | data formatting | bytes 16777216 | tf_op jit(solution)/shard_map/concatenate | solution.py:31
  324.6 9.3 %reshape.213 = f32[1,64,32768]{2,1,0:T(8,128)} reshape(f32[1,64,128,256]{3,2,1,0:T(8,128)} %copy.68) | data formatting | bytes 16777216 | tf_op jit(solution)/shard_map/reshape | solution.py:32
  333.9 7.1 %slice.78 = f32[1,64,32639]{2,1,0:T(8,128)} slice(f32[1,64,32768]{2,1,0:T(8,128)} %reshape.213), slice={[0:1], [0:64], [0:32639]} | slice | bytes 16711168 | tf_op jit(solution)/shard_map/slice | solution.py:35
  341.0 14.0 %reshape.214 = f32[1,64,127,257]{3,2,1,0:T(8,128)} reshape(f32[1,64,32639]{2,1,0:T(8,128)} %slice.78) | data formatting | bytes 16711168 | tf_op jit(solution)/shard_map/reshape | solution.py:36
  355.0 7.7 %pad_maximum_fusion.3 = f32[1,64,128,256]{2,3,1,0:T(8,128)} fusion(f32[1,64,128,128]{2,3,1,0:T(8,128)} %convolution_bitcast_fusion.2), kind=kLoop, calls=%fused_computation.3 | loop fusion | flops 2097152 | bytes 12582912 | tf_op jit(solution)/shard_map/concatenate | solution.py:31
  362.7 9.0 %copy.77 = f32[1,64,128,256]{3,2,1,0:T(8,128)} copy(f32[1,64,128,256]{2,3,1,0:T(8,128)} %pad_maximum_fusion.3) | data formatting | bytes 16777216 | tf_op jit(solution)/shard_map/concatenate | solution.py:31
  371.6 9.4 %reshape.221 = f32[1,64,32768]{2,1,0:T(8,128)} reshape(f32[1,64,128,256]{3,2,1,0:T(8,128)} %copy.77) | data formatting | bytes 16777216 | tf_op jit(solution)/shard_map/reshape | solution.py:32
  381.1 7.1 %slice.87 = f32[1,64,32639]{2,1,0:T(8,128)} slice(f32[1,64,32768]{2,1,0:T(8,128)} %reshape.221), slice={[0:1], [0:64], [0:32639]} | slice | bytes 16711168 | tf_op jit(solution)/shard_map/slice | solution.py:35
  388.2 14.0 %reshape.222 = f32[1,64,127,257]{3,2,1,0:T(8,128)} reshape(f32[1,64,32639]{2,1,0:T(8,128)} %slice.87) | data formatting | bytes 16711168 | tf_op jit(solution)/shard_map/reshape | solution.py:36
  402.2 7.7 %pad_maximum_fusion.4 = f32[1,64,128,256]{2,3,1,0:T(8,128)} fusion(f32[1,64,128,128]{2,3,1,0:T(8,128)} %convolution_bitcast_fusion.1), kind=kLoop, calls=%fused_computation.4 | loop fusion | flops 2097152 | bytes 12582912 | tf_op jit(solution)/shard_map/concatenate | solution.py:31
  409.9 9.0 %copy.80 = f32[1,64,128,256]{3,2,1,0:T(8,128)} copy(f32[1,64,128,256]{2,3,1,0:T(8,128)} %pad_maximum_fusion.4) | data formatting | bytes 16777216 | tf_op jit(solution)/shard_map/concatenate | solution.py:31
  418.9 9.3 %reshape.223 = f32[1,64,32768]{2,1,0:T(8,128)} reshape(f32[1,64,128,256]{3,2,1,0:T(8,128)} %copy.80) | data formatting | bytes 16777216 | tf_op jit(solution)/shard_map/reshape | solution.py:32
  428.2 7.1 %slice.90 = f32[1,64,32639]{2,1,0:T(8,128)} slice(f32[1,64,32768]{2,1,0:T(8,128)} %reshape.223), slice={[0:1], [0:64], [0:32639]} | slice | bytes 16711168 | tf_op jit(solution)/shard_map/slice | solution.py:35
  435.3 14.3 %reshape.224 = f32[1,64,127,257]{3,2,1,0:T(8,128)} reshape(f32[1,64,32639]{2,1,0:T(8,128)} %slice.90) | data formatting | bytes 16711168 | tf_op jit(solution)/shard_map/reshape | solution.py:36
  453.1 3.8 pad_maximum_fusion.2
  456.8 9.0 %copy.74 = f32[1,64,128,256]{3,2,1,0:T(8,128)} copy(f32[1,64,128,256]{2,3,1,0:T(8,128)} %pad_maximum_fusion.2) | data formatting | bytes 16777216 | tf_op jit(solution)/shard_map/concatenate | solution.py:31
  465.8 9.4 %reshape.219 = f32[1,64,32768]{2,1,0:T(8,128)} reshape(f32[1,64,128,256]{3,2,1,0:T(8,128)} %copy.74) | data formatting | bytes 16777216 | tf_op jit(solution)/shard_map/reshape | solution.py:32
  475.2 7.1 %slice.84 = f32[1,64,32639]{2,1,0:T(8,128)} slice(f32[1,64,32768]{2,1,0:T(8,128)} %reshape.219), slice={[0:1], [0:64], [0:32639]} | slice | bytes 16711168 | tf_op jit(solution)/shard_map/slice | solution.py:35
  482.3 14.1 %reshape.220 = f32[1,64,127,257]{3,2,1,0:T(8,128)} reshape(f32[1,64,32639]{2,1,0:T(8,128)} %slice.84) | data formatting | bytes 16711168 | tf_op jit(solution)/shard_map/reshape | solution.py:36
  499.9 3.8 pad_maximum_fusion.1
  503.6 9.0 %copy.71 = f32[1,64,128,256]{3,2,1,0:T(8,128)} copy(f32[1,64,128,256]{2,3,1,0:T(8,128)} %pad_maximum_fusion.1) | data formatting | bytes 16777216 | tf_op jit(solution)/shard_map/concatenate | solution.py:31
  512.6 9.4 %reshape.216 = f32[1,64,32768]{2,1,0:T(8,128)} reshape(f32[1,64,128,256]{3,2,1,0:T(8,128)} %copy.71) | data formatting | bytes 16777216 | tf_op jit(solution)/shard_map/reshape | solution.py:32
  522.0 7.1 %slice.81 = f32[1,64,32639]{2,1,0:T(8,128)} slice(f32[1,64,32768]{2,1,0:T(8,128)} %reshape.216), slice={[0:1], [0:64], [0:32639]} | slice | bytes 16711168 | tf_op jit(solution)/shard_map/slice | solution.py:35
  529.2 14.1 %reshape.217 = f32[1,64,127,257]{3,2,1,0:T(8,128)} reshape(f32[1,64,32639]{2,1,0:T(8,128)} %slice.81) | data formatting | bytes 16711168 | tf_op jit(solution)/shard_map/reshape | solution.py:36
  546.7 3.8 pad_maximum_fusion.5
  550.5 9.0 %copy.83 = f32[1,64,128,256]{3,2,1,0:T(8,128)} copy(f32[1,64,128,256]{2,3,1,0:T(8,128)} %pad_maximum_fusion.5) | data formatting | bytes 16777216 | tf_op jit(solution)/shard_map/concatenate | solution.py:31
  559.5 9.4 %reshape.225 = f32[1,64,32768]{2,1,0:T(8,128)} reshape(f32[1,64,128,256]{3,2,1,0:T(8,128)} %copy.83) | data formatting | bytes 16777216 | tf_op jit(solution)/shard_map/reshape | solution.py:32
  568.9 7.1 %slice.93 = f32[1,64,32639]{2,1,0:T(8,128)} slice(f32[1,64,32768]{2,1,0:T(8,128)} %reshape.225), slice={[0:1], [0:64], [0:32639]} | slice | bytes 16711168 | tf_op jit(solution)/shard_map/slice | solution.py:35
  576.0 14.3 %reshape.226 = f32[1,64,127,257]{3,2,1,0:T(8,128)} reshape(f32[1,64,32639]{2,1,0:T(8,128)} %slice.93) | data formatting | bytes 16711168 | tf_op jit(solution)/shard_map/reshape | solution.py:36
  592.9 4.6 slice_reduce_fusion.2
  (48 shorter events, 40.0 us)
Async XLA Ops:
  0.6 37.4 %copy-start.11 = (s32[1,1,64]{2,1,0:T(1,128)S(1)}, s32[1,1,64]{2,1,0:T(1,128)}, u32[]{:S(2)}) copy-start(s32[1,1,64]{2,1,0:T(1,128)} %param.4) | copy-start | bytes 772
  0.6 37.5 %copy-start.9 = (s32[1,1,64]{2,1,0:T(1,128)S(1)}, s32[1,1,64]{2,1,0:T(1,128)}, u32[]{:S(2)}) copy-start(s32[1,1,64]{2,1,0:T(1,128)} %param.5) | copy-start | bytes 772
  32.5 27.7 %collective-permute-start = (bf16[128,8192]{0,1:T(8,128)(2,1)}, bf16[128,8192]{0,1:T(8,128)(2,1)}, u32[]{:S(2)}, u32[]{:S(2)}) collective-permute-start(bf16[128,8192]{0,1:T(8,128)(2,1)} %bitcast.126), channel_id=1, source_target_pairs={{0,1},{1,2},{2,3},{3,4},{4,5},{5,6},{6,7},{7,8},{8,9},{9,10},{10,1... | collective-permute-start | bytes 6291464 | tf_op jit(solution)/shard_map/ppermute | solution.py:14
  35.1 29.1 %collective-permute-start.1 = (bf16[128,8192]{0,1:T(8,128)(2,1)}, bf16[128,8192]{0,1:T(8,128)(2,1)}, u32[]{:S(2)}, u32[]{:S(2)}) collective-permute-start(bf16[128,8192]{0,1:T(8,128)(2,1)} %bitcast.127), channel_id=1, source_target_pairs={{1,0},{2,1},{3,2},{4,3},{5,4},{6,5},{7,6},{8,7},{9,8},{10,9},{11,1... | collective-permute-start | bytes 6291464 | tf_op jit(solution)/shard_map/ppermute | solution.py:17
  73.4 95.0 %collective-permute-start.2 = (bf16[1,128,64,128]{3,2,1,0:T(8,128)(2,1)S(1)}, bf16[1,128,64,128]{3,2,1,0:T(8,128)(2,1)S(1)}, u32[]{:S(2)}, u32[]{:S(2)}) collective-permute-start(bf16[1,128,64,128]{3,2,1,0:T(8,128)(2,1)S(1)} %bitcast.114), channel_id=1, source_target_pairs={{0,16},{16,32},{32,48},{48,64},{64,80},{80,96},{96,112},{1,17},{17... | collective-permute-start | bytes 6291464 | tf_op jit(solution)/shard_map/ppermute | solution.py:25
  76.9 97.0 %collective-permute-start.3 = (bf16[1,128,64,128]{3,2,1,0:T(8,128)(2,1)S(1)}, bf16[1,128,64,128]{3,2,1,0:T(8,128)(2,1)}, u32[]{:S(2)}, u32[]{:S(2)}) collective-permute-start(bf16[1,128,64,128]{3,2,1,0:T(8,128)(2,1)S(1)} %bitcast.115), channel_id=1, source_target_pairs={{0,32},{16,48},{32,64},{48,80},{64,96},{80,112},{1,33},{17,49},{33... | collective-permute-start | bytes 6291464 | tf_op jit(solution)/shard_map/ppermute | solution.py:25
  78.2 218.9 %collective-permute-start.4 = (bf16[1,128,64,128]{3,2,1,0:T(8,128)(2,1)S(1)}, bf16[1,128,64,128]{3,2,1,0:T(8,128)(2,1)}, u32[]{:S(2)}, u32[]{:S(2)}) collective-permute-start(bf16[1,128,64,128]{3,2,1,0:T(8,128)(2,1)S(1)} %bitcast.116), channel_id=1, source_target_pairs={{0,48},{16,64},{32,80},{48,96},{64,112},{1,49},{17,65},{33,81},{49... | collective-permute-start | bytes 6291464 | tf_op jit(solution)/shard_map/ppermute | solution.py:25
  168.4 1.3 copy-start.7
  178.1 6.1 %copy-start.1 = (bf16[128,64,128]{0,2,1:T(8,128)(2,1)S(1)}, bf16[128,64,128]{0,2,1:T(8,128)(2,1)}, u32[]{:S(2)}) copy-start(bf16[128,64,128]{0,2,1:T(8,128)(2,1)} %copy.79) | copy-start | bytes 6291460
  184.1 4.4 copy-start
  301.4 6.1 %copy-start.2 = (bf16[128,64,128]{0,2,1:T(8,128)(2,1)S(1)}, bf16[128,64,128]{0,2,1:T(8,128)(2,1)}, u32[]{:S(2)}) copy-start(bf16[128,64,128]{0,2,1:T(8,128)(2,1)} %copy.82) | copy-start | bytes 6291460
  307.5 4.3 copy-start.6
  449.6 3.5 copy-start.5
  496.4 3.5 copy-start.4
  543.2 3.5 copy-start.3
  597.6 4.5 copy-start.8
  597.6 5.1 copy-start.10
where the time goes:
time: 615 us; the launch traced here: 606 us
  local copies, waits for them, and re-layouts  271 us (44%)
  waiting for transfers between devices  203 us (33%)
  other arithmetic  54.5 us (9%)
  matrix products  34.5 us (6%)
  blocking collectives  29.4 us (5%)
  starting transfers between devices  12.2 us (2%)
    ppermute x3, waiting for transfers between devices, from_behind(): return lax.ppermute(block, axis, route)  188 us
    reshape x6, local copies, waits for them, and re-layouts, lag_profile(): upper_part = flattened[..., :(block_len - 1) * stride].reshape(leading +...  84.8 us
    reshape x6, local copies, waits for them, and re-layouts, lag_profile(): flattened = doubled.reshape(leading + (2 * block_len * block_len,))  56.2 us
    concatenate x6, local copies, waits for them, and re-layouts, lag_profile(): doubled = jnp.concatenate([matrix, matrix], -1)  54 us
    slice x6, local copies, waits for them, and re-layouts, lag_profile(): flattened[..., :(block_len - 1) * stride]  42.7 us
    concatenate x6, other arithmetic, lag_profile(): doubled = jnp.concatenate([matrix, matrix], -1)  30.4 us
    all_to_all x1, blocking collectives, body(): lax.all_to_all(column, 'row', split_axis=0, concat_axis=1, tiled=True)  29.4 us
    dot_general x3, matrix products, pair_scores(): jnp.einsum('bpjq,bsjq->bjps', current, previous, preferred_element_type=j...  16.5 us
  transfers between devices with their start and end apart: 5, of which 3 were waited for; matrix products, arithmetic and copies ran while one was open for 6% of the time, Pallas kernels for 0%

commit v1 on v0

v1 whole, which is shorter than its diff:
```python
import functools

import jax
import jax.numpy as jnp
from jax import lax
from jax.experimental import pallas as pl
from jax.experimental.pallas import tpu as pltpu
from jax.sharding import PartitionSpec as P

BLOCK = 128
LAGS = 3


def warp_kernel(shifts, columns, up, own, down, out, sem):
    blocks = out.shape[0]
    width = own.shape[2] // BLOCK

    @pl.loop(0, blocks)
    def _(j):
        column = columns[j]
        stripe = column // width
        lane = pl.multiple_of((column % width) * BLOCK, BLOCK)
        shift = shifts[j]
        for step, source in ((-1, up), (0, own), (1, down)):

            @pl.when(shift == step)
            def _():
                pltpu.make_async_copy(
                    source.at[stripe, :, pl.ds(lane, BLOCK)], out.at[j], sem
                ).start()

    pltpu.make_async_copy(out, out, sem).wait()


def warp(shifts, columns, up, own, down):
    blocks = shifts.shape[0]
    return pl.pallas_call(
        warp_kernel,
        grid_spec=pltpu.PrefetchScalarGridSpec(
            num_scalar_prefetch=2,
            grid=(1,),
            in_specs=[pl.BlockSpec(memory_space=pl.ANY)] * 3,
            out_specs=pl.BlockSpec(memory_space=pl.ANY),
            scratch_shapes=[pltpu.SemaphoreType.DMA],
        ),
        out_shape=jax.ShapeDtypeStruct((blocks, BLOCK, BLOCK), jnp.bfloat16),
        name="warp",
    )(shifts, columns, up, own, down)


def lag_sums(matrix):
    total = matrix[0:8]
    for start in range(8, BLOCK, 8):
        total = total + pltpu.roll(matrix[start : start + 8], BLOCK - start, axis=1)
    for half in (4, 2, 1):
        upper = pltpu.roll(total, 8 - half, axis=0)
        total = total + pltpu.roll(upper, BLOCK - half, axis=1)
    return total[0:1]


def score_kernel(blocks, out, flipped):
    sections = blocks.shape[0]
    place = pl.ds(pl.program_id(0), 1)
    energies = []
    for s in range(sections):
        block = blocks[s, 0]
        flipped[s] = block.T
        values = block.astype(jnp.float32)
        energies.append(
            jnp.sum(jnp.sum(values * values, axis=0, keepdims=True), axis=1, keepdims=True)
            / (BLOCK * BLOCK)
        )
    for s in range(min(LAGS, sections)):
        for k in range(s + 1, LAGS + 1):
            out[s, 0, k - 1, place, :] = jnp.zeros((1, BLOCK), jnp.float32)
            out[s, 1, k - 1, place, :] = jnp.zeros((1, BLOCK), jnp.float32)
    for back in range(sections - 1):
        count = min(LAGS, sections - 1 - back)
        previous = blocks[back, 0]
        current = blocks[back + 1 : back + 1 + count, 0].reshape(count * BLOCK, BLOCK)
        current_flipped = flipped[back + 1 : back + 1 + count].reshape(count * BLOCK, BLOCK)
        row_corr = jnp.dot(current, flipped[back], preferred_element_type=jnp.float32)
        col_corr = jnp.dot(current_flipped, previous, preferred_element_type=jnp.float32)
        for k in range(1, count + 1):
            s = back + k
            scaling = 1.0 / (BLOCK * jnp.sqrt(energies[s] * energies[back] + 1e-06))
            part = slice((k - 1) * BLOCK, k * BLOCK)
            out[s, 0, k - 1, place, :] = lag_sums(row_corr[part]) * scaling
            out[s, 1, k - 1, place, :] = lag_sums(col_corr[part]) * scaling


def scores(blocks):
    sections, columns = blocks.shape[:2]
    shape = (sections, 2, LAGS, columns, BLOCK)
    pairs = LAGS * sections - LAGS * (LAGS + 1) // 2
    return pl.pallas_call(
        score_kernel,
        grid=(columns,),
        in_specs=[pl.BlockSpec((sections, 1, BLOCK, BLOCK), lambda j: (0, j, 0, 0))],
        out_specs=pl.BlockSpec(shape, lambda j: (0, 0, 0, 0, 0)),
        out_shape=jax.ShapeDtypeStruct(shape, jnp.float32),
        scratch_shapes=[pltpu.VMEM((sections, BLOCK, BLOCK), jnp.bfloat16)],
        compiler_params=pltpu.CompilerParams(vmem_limit_bytes=32 * 1024 * 1024),
        cost_estimate=pl.CostEstimate(
            flops=4 * columns * pairs * BLOCK**3, bytes_accessed=2 * blocks.size, transcendentals=0
        ),
        name="scores",
    )(blocks)


def body(raw_sections, shift_rows, source_cols):
    raw = raw_sections[0]
    rows = lax.axis_size("row")
    sections = lax.axis_size("sec")
    stripes = lax.all_to_all(
        raw.reshape(rows, -1, raw.shape[1]), "row", split_axis=0, concat_axis=0, tiled=True
    )
    forward = [(i, i + 1) for i in range(rows - 1)]
    backward = [(target, source) for source, target in forward]
    up = lax.ppermute(stripes, "row", forward)
    down = lax.ppermute(stripes, "row", backward)
    warped = warp(shift_rows[0, 0], source_cols[0, 0], up, stripes, down)
    warped = warped.reshape(sections, -1, BLOCK, BLOCK)
    chunk = lax.all_to_all(warped, "sec", split_axis=0, concat_axis=0, tiled=True)
    result = scores(chunk)
    result = lax.all_to_all(result, "sec", split_axis=0, concat_axis=0, tiled=True)
    result = result.transpose(1, 2, 0, 3, 4).reshape(2, 1, LAGS, 1, -1, BLOCK)
    return result[0], result[1]


def solution(mesh):
    return jax.shard_map(
        body,
        mesh=mesh,
        in_specs=(P("sec", None, "row"), P("sec", "row", None), P("sec", "row", None)),
        out_specs=(P("sec", None, "row", None, None), P("sec", None, "row", None, None)),
        check_vma=False,
    )
```

time: 615 us -> 209 us (0.34)
  the two profiles are of different devices: /device:TPU:84 before, /device:TPU:25 now
where the time goes in v1:
time: 209 us; the launch traced here: 207 us
  Pallas kernels  97 us (46%)
  blocking collectives  76.8 us (37%)
  waiting for transfers between devices  23 us (11%)
  starting transfers between devices  7.66 us (4%)
  local copies, waits for them, and re-layouts  2.19 us (1%)
    pallas_call x1, Pallas kernels, warp(): pl.pallas_call(warp_kernel, grid_spec=pltpu.PrefetchScalarGridSpec(num_sc...  65.3 us
    all_to_all x1, blocking collectives, body(): lax.all_to_all(warped, 'sec', split_axis=0, concat_axis=0, tiled=True)  35 us
    all_to_all x1, blocking collectives, body(): lax.all_to_all(raw.reshape(rows, -1, raw.shape[1]), 'row', split_axis=0,...  31.7 us
    pallas_call x1, Pallas kernels, scores(): pl.pallas_call(score_kernel, grid=(columns,), in_specs=[pl.BlockSpec((sec...  31.7 us
    ppermute x1, waiting for transfers between devices, body(): down = lax.ppermute(stripes, 'row', backward)  21.8 us
    all_to_all x1, blocking collectives, body(): lax.all_to_all(result, 'sec', split_axis=0, concat_axis=0, tiled=True)  10.1 us
    ppermute x1, starting transfers between devices, body(): up = lax.ppermute(stripes, 'row', forward)  5.55 us
  transfers between devices with their start and end apart: 2, of which 2 were waited for; matrix products, arithmetic and copies ran while one was open for 0% of the time, Pallas kernels for 0%

profile of v1, /device:TPU:25, one launch (start us, length us, event | category | flops | bytes accessed | tf_op | source)
XLA Modules:
  0.0 207.3 jit_solution(6157457460573109707)
XLA Ops:
  0.6 31.7 %all_to_all.15.own = bf16[16,128,512]{2,1,0:T(8,128)(2,1)S(1)} all-to-all(bf16[16,128,512]{2,1,0:T(8,128)(2,1)} %bitcast.14), channel_id=1, replica_groups=mesh['sec'=8,'row'=16] {'row'}, dimensions={0} | all-to-all | bytes 4194304 | tf_op jit(solution)/shard_map/all_to_all | solution.py:115
  32.3 0.0 copy-start
  32.3 2.1 %collective-permute-start.1 = (bf16[16,128,512]{2,1,0:T(8,128)(2,1)S(1)}, bf16[16,128,512]{2,1,0:T(8,128)(2,1)S(1)}, u32[]{:S(2)}, u32[]{:S(2)}) collective-permute-start(bf16[16,128,512]{2,1,0:T(8,128)(2,1)S(1)} %all_to_all.15.own), channel_id=1, source_target_pairs={{1,0},{2,1},{3,2},{4,3},{5,4},{6,5},{7,6},{8,7},{9,8},{10,9},{11,1... | collective-permute-start | bytes 6291464 | tf_op jit(solution)/shard_map/ppermute | solution.py:121
  34.4 5.6 %collective-permute-start = (bf16[16,128,512]{2,1,0:T(8,128)(2,1)S(1)}, bf16[16,128,512]{2,1,0:T(8,128)(2,1)S(1)}, u32[]{:S(2)}, u32[]{:S(2)}) collective-permute-start(bf16[16,128,512]{2,1,0:T(8,128)(2,1)S(1)} %all_to_all.15.own), channel_id=1, source_target_pairs={{0,1},{1,2},{2,3},{3,4},{4,5},{5,6},{6,7},{7,8},{8,9},{9,10},{10,1... | collective-permute-start | bytes 6291464 | tf_op jit(solution)/shard_map/ppermute | solution.py:120
  40.0 21.8 %collective-permute-done.1.down = bf16[16,128,512]{2,1,0:T(8,128)(2,1)S(1)} collective-permute-done((bf16[16,128,512]{2,1,0:T(8,128)(2,1)S(1)}, bf16[16,128,512]{2,1,0:T(8,128)(2,1)S(1)}, u32[]{:S(2)}, u32[]{:S(2)}) %collective-permute-start.1) | collective-permute-done | bytes 2097184 | tf_op jit(solution)/shard_map/ppermute | solution.py:121
  61.7 0.0 copy-start.1
  61.7 1.2 collective-permute-done.up
  62.9 0.1 copy-done.1
  63.1 0.0 copy-start.2
  63.1 1.4 copy-done.2
  64.4 0.0 copy-done
  64.4 65.3 %warp.1 = bf16[64,128,128]{2,1,0:T(8,128)(2,1)} custom-call(s32[64]{0:T(128)} %bitcast.16, s32[64]{0:T(128)} %bitcast.17, bf16[16,128,512]{2,1,0:T(8,128)(2,1)} %copy-done.2, bf16[16,128,512]{2,1,0:T(8,128)(2,1)} %copy-done, bf16[16,128,512]{2,1,0:T(8,128)(2,1)} %copy-done.1), custom_call_target="tpu_custom_call" | custom-call | tf_op jit(solution)/shard_map/warp/pallas_call | solution.py:37
  129.7 35.0 %all_to_all.16.blocks = bf16[8,8,128,128]{3,2,1,0:T(8,128)(2,1)S(1)} all-to-all(bf16[8,8,128,128]{3,2,1,0:T(8,128)(2,1)} %bitcast.13), channel_id=1, replica_groups=mesh['sec'=8,'row'=16] {'sec'}, dimensions={0} | all-to-all | bytes 4194304 | tf_op jit(solution)/shard_map/all_to_all | solution.py:124
  164.8 31.7 %scores.1 = f32[8,2,3,8,128]{4,3,2,1,0:T(8,128)S(1)} custom-call(bf16[8,8,128,128]{3,2,1,0:T(8,128)(2,1)S(1)} %all_to_all.16.blocks), custom_call_target="tpu_custom_call" | custom-call | flops 1207959552 | bytes 2097152 | tf_op jit(solution)/shard_map/scores/pallas_call | solution.py:96
  196.4 10.1 %all_to_all.17 = f32[8,2,3,8,128]{4,3,2,1,0:T(8,128)S(1)} all-to-all(f32[8,2,3,8,128]{4,3,2,1,0:T(8,128)S(1)} %scores.1), channel_id=1, replica_groups=mesh['sec'=8,'row'=16] {'sec'}, dimensions={0} | all-to-all | bytes 393216 | tf_op jit(solution)/shard_map/all_to_all | solution.py:126
  206.6 0.7 copy_bitcast_fusion
  (1 shorter events, 0.0 us)
Async XLA Ops:
  32.3 32.1 %copy-start = (bf16[16,128,512]{2,1,0:T(8,128)(2,1)}, bf16[16,128,512]{2,1,0:T(8,128)(2,1)S(1)}, u32[]{:S(2)}) copy-start(bf16[16,128,512]{2,1,0:T(8,128)(2,1)S(1)} %all_to_all.15.own) | copy-start | bytes 6291460
  32.3 29.5 %collective-permute-start.1 = (bf16[16,128,512]{2,1,0:T(8,128)(2,1)S(1)}, bf16[16,128,512]{2,1,0:T(8,128)(2,1)S(1)}, u32[]{:S(2)}, u32[]{:S(2)}) collective-permute-start(bf16[16,128,512]{2,1,0:T(8,128)(2,1)S(1)} %all_to_all.15.own), channel_id=1, source_target_pairs={{1,0},{2,1},{3,2},{4,3},{5,4},{6,5},{7,6},{8,7},{9,8},{10,9},{11,1... | collective-permute-start | bytes 6291464 | tf_op jit(solution)/shard_map/ppermute | solution.py:121
  34.4 28.5 %collective-permute-start = (bf16[16,128,512]{2,1,0:T(8,128)(2,1)S(1)}, bf16[16,128,512]{2,1,0:T(8,128)(2,1)S(1)}, u32[]{:S(2)}, u32[]{:S(2)}) collective-permute-start(bf16[16,128,512]{2,1,0:T(8,128)(2,1)S(1)} %all_to_all.15.own), channel_id=1, source_target_pairs={{0,1},{1,2},{2,3},{3,4},{4,5},{5,6},{6,7},{7,8},{8,9},{9,10},{10,1... | collective-permute-start | bytes 6291464 | tf_op jit(solution)/shard_map/ppermute | solution.py:120
  61.7 1.3 copy-start.1
  63.1 1.4 copy-start.2

commit v2 on v1

v2 whole, which is shorter than its diff:
```python
import functools

import jax
import jax.numpy as jnp
from jax import lax
from jax.experimental import pallas as pl
from jax.experimental.pallas import tpu as pltpu
from jax.sharding import PartitionSpec as P

BLOCK = 128
LAGS = 3


def warp_kernel(shifts, columns, up, own, down, out):
    width = own.shape[2] // BLOCK

    @pl.loop(0, out.shape[0], unroll=4)
    def _(j):
        column = columns[j]
        stripe = column // width
        lane = pl.multiple_of((column % width) * BLOCK, BLOCK)
        shift = shifts[j]
        for step, source in ((-1, up), (0, own), (1, down)):

            @pl.when(shift == step)
            def _():
                out[j] = source[stripe, :, pl.ds(lane, BLOCK)]


def warp(shifts, columns, up, own, down):
    shape = (shifts.shape[0], BLOCK, BLOCK)
    return pl.pallas_call(
        warp_kernel,
        in_specs=[pl.BlockSpec(memory_space=pltpu.SMEM)] * 2
        + [pl.BlockSpec(memory_space=pltpu.VMEM)] * 3,
        out_specs=pl.BlockSpec(memory_space=pltpu.VMEM),
        out_shape=jax.ShapeDtypeStruct(shape, jnp.bfloat16),
        compiler_params=pltpu.CompilerParams(vmem_limit_bytes=16 * 1024 * 1024),
        cost_estimate=pl.CostEstimate(
            flops=0, bytes_accessed=8 * own.size, transcendentals=0
        ),
        name="warp",
    )(shifts, columns, up, own, down)


def partial_lags(matrix):
    total = matrix[0:8]
    for start in range(8, matrix.shape[0], 8):
        total = total + pltpu.roll(matrix[start : start + 8], BLOCK - start, axis=1)
    return total


def halves(block):
    return jnp.concatenate([block[: BLOCK // 2], block[BLOCK // 2 :]], axis=1)


def turned(block):
    return jnp.concatenate([block[BLOCK // 2 :], block[: BLOCK // 2]], axis=0)


def score_kernel(blocks, out, flipped, by_row, by_column, lags, squares):
    sections = blocks.shape[0]
    steps = out.shape[3]
    place = pl.ds(pl.multiple_of(pl.program_id(0) * 8, 8), 8)
    for s in range(sections):
        block = blocks[s, 0]
        flip = block.T
        flipped[s] = flip
        by_row[s, :BLOCK] = flip
        by_row[s, BLOCK:] = turned(block).T
        by_column[s, :BLOCK] = block
        by_column[s, BLOCK:] = pltpu.roll(block, BLOCK // 2, axis=1)
        values = block.astype(jnp.float32)
        values = values * values
        total = values[0:8]
        for start in range(8, BLOCK, 8):
            total = total + values[start : start + 8]
        squares[s, place, :] = total
    for back in range(sections - 1):
        count = min(LAGS, sections - 1 - back)
        near = range(back + 1, back + 1 + count)
        current = jnp.concatenate([halves(blocks[s, 0]) for s in near], axis=0)
        current_flipped = jnp.concatenate([halves(flipped[s]) for s in near], axis=0)
        row_corr = jnp.dot(current, by_row[back], preferred_element_type=jnp.float32)
        col_corr = jnp.dot(current_flipped, by_column[back], preferred_element_type=jnp.float32)
        for k in range(count):
            part = slice(k * BLOCK // 2, (k + 1) * BLOCK // 2)
            lags[back + 1 + k, 0, k, place, :] = partial_lags(row_corr[part])
            lags[back + 1 + k, 1, k, place, :] = partial_lags(col_corr[part])

    @pl.when(pl.program_id(0) == steps - 1)
    def _():
        energies = []
        for s in range(sections):
            total = squares[s, pl.ds(0, steps, stride=8), :]
            for b in range(1, 8):
                total = total + squares[s, pl.ds(b, steps, stride=8), :]
            energies.append(jnp.sum(total, axis=1, keepdims=True) / (BLOCK * BLOCK))
        for s in range(sections):
            for k in range(1, LAGS + 1):
                if s < k:
                    for way in range(2):
                        out[s, way, k - 1] = jnp.zeros((steps, BLOCK), jnp.float32)
                    continue
                scaling = 1.0 / (BLOCK * jnp.sqrt(energies[s] * energies[s - k] + 1e-06))
                for way in range(2):
                    total = lags[s, way, k - 1, pl.ds(0, steps, stride=8), :]
                    for b in range(1, 8):
                        row = lags[s, way, k - 1, pl.ds(b, steps, stride=8), :]
                        total = total + pltpu.roll(row, BLOCK - b, axis=1)
                    out[s, way, k - 1] = total * scaling


def scores(blocks):
    sections, columns = blocks.shape[:2]
    shape = (sections, 2, LAGS, columns, BLOCK)
    pairs = LAGS * sections - LAGS * (LAGS + 1) // 2
    return pl.pallas_call(
        score_kernel,
        grid=(columns,),
        in_specs=[pl.BlockSpec((sections, 1, BLOCK, BLOCK), lambda j: (0, j, 0, 0))],
        out_specs=pl.BlockSpec(shape, lambda j: (0, 0, 0, 0, 0)),
        out_shape=jax.ShapeDtypeStruct(shape, jnp.float32),
        scratch_shapes=[
            pltpu.VMEM((sections, BLOCK, BLOCK), jnp.bfloat16),
            pltpu.VMEM((sections, 2 * BLOCK, BLOCK), jnp.bfloat16),
            pltpu.VMEM((sections, 2 * BLOCK, BLOCK), jnp.bfloat16),
            pltpu.VMEM((sections, 2, LAGS, columns * 8, BLOCK), jnp.float32),
            pltpu.VMEM((sections, columns * 8, BLOCK), jnp.float32),
        ],
        compiler_params=pltpu.CompilerParams(vmem_limit_bytes=16 * 1024 * 1024),
        cost_estimate=pl.CostEstimate(
            flops=4 * columns * pairs * BLOCK**3, bytes_accessed=2 * blocks.size, transcendentals=0
        ),
        name="scores",
    )(blocks)


def body(raw_sections, shift_rows, source_cols):
    raw = raw_sections[0]
    rows = lax.axis_size("row")
    sections = lax.axis_size("sec")
    stripes = lax.all_to_all(
        raw.reshape(rows, -1, raw.shape[1]), "row", split_axis=0, concat_axis=0, tiled=True
    )
    forward = [(i, i + 1) for i in range(rows - 1)]
    backward = [(target, source) for source, target in forward]
    up = lax.ppermute(stripes, "row", forward)
    down = lax.ppermute(stripes, "row", backward)
    warped = warp(shift_rows[0, 0], source_cols[0, 0], up, stripes, down)
    warped = warped.reshape(sections, -1, BLOCK, BLOCK)
    chunk = lax.all_to_all(warped, "sec", split_axis=0, concat_axis=0, tiled=True)
    result = scores(chunk)
    result = lax.all_to_all(result, "sec", split_axis=0, concat_axis=0, tiled=True)
    result = result.transpose(1, 2, 0, 3, 4).reshape(2, 1, LAGS, 1, -1, BLOCK)
    return result[0], result[1]


def solution(mesh):
    return jax.shard_map(
        body,
        mesh=mesh,
        in_specs=(P("sec", None, "row"), P("sec", "row", None), P("sec", "row", None)),
        out_specs=(P("sec", None, "row", None, None), P("sec", None, "row", None, None)),
        check_vma=False,
    )
```

time: 209 us -> 119 us (0.57)
  Pallas kernels: 97 us -> 8.48 us
    pallas_call x1, Pallas kernels: 65.3 us -> 2.36 us  [warp(): pl.pallas_call(warp_kernel, in_specs=[pl.BlockSpec(memory_space=pltpu.SME...]
    pallas_call x1, Pallas kernels: 31.7 us -> 6.12 us  [scores(): pl.pallas_call(score_kernel, grid=(columns,), in_specs=[pl.BlockSpec((sec...]
where the time goes in v2:
time: 119 us; the launch traced here: 117 us
  blocking collectives  76.7 us (64%)
  waiting for transfers between devices  23 us (19%)
  Pallas kernels  8.48 us (7%)
  starting transfers between devices  7.66 us (6%)
    all_to_all x1, blocking collectives, body(): lax.all_to_all(warped, 'sec', split_axis=0, concat_axis=0, tiled=True)  34.9 us
    all_to_all x1, blocking collectives, body(): lax.all_to_all(raw.reshape(rows, -1, raw.shape[1]), 'row', split_axis=0,...  31.7 us
    ppermute x1, waiting for transfers between devices, body(): down = lax.ppermute(stripes, 'row', backward)  21.8 us
    all_to_all x1, blocking collectives, body(): lax.all_to_all(result, 'sec', split_axis=0, concat_axis=0, tiled=True)  10.2 us
    pallas_call x1, Pallas kernels, scores(): pl.pallas_call(score_kernel, grid=(columns,), in_specs=[pl.BlockSpec((sec...  6.12 us
    ppermute x1, starting transfers between devices, body(): up = lax.ppermute(stripes, 'row', forward)  5.55 us
  transfers between devices with their start and end apart: 2, of which 2 were waited for; matrix products, arithmetic and copies ran while one was open for 0% of the time, Pallas kernels for 0%

profile of v2, /device:TPU:25, one launch (start us, length us, event | category | flops | bytes accessed | tf_op | source)
XLA Modules:
  0.0 117.2 jit_solution(7552951049306421423)
XLA Ops:
  0.6 0.0 copy-start
  0.6 0.0 copy-start.1
  0.6 31.7 %all_to_all.15.own = bf16[16,128,512]{2,1,0:T(8,128)(2,1)S(1)} all-to-all(bf16[16,128,512]{2,1,0:T(8,128)(2,1)} %bitcast.16), channel_id=1, replica_groups=mesh['sec'=8,'row'=16] {'row'}, dimensions={0} | all-to-all | bytes 4194304 | tf_op jit(solution)/shard_map/all_to_all | solution.py:143
  32.3 2.1 %collective-permute-start.1 = (bf16[16,128,512]{2,1,0:T(8,128)(2,1)S(1)}, bf16[16,128,512]{2,1,0:T(8,128)(2,1)S(1)}, u32[]{:S(2)}, u32[]{:S(2)}) collective-permute-start(bf16[16,128,512]{2,1,0:T(8,128)(2,1)S(1)} %all_to_all.15.own), channel_id=1, source_target_pairs={{1,0},{2,1},{3,2},{4,3},{5,4},{6,5},{7,6},{8,7},{9,8},{10,9},{11,1... | collective-permute-start | bytes 6291464 | tf_op jit(solution)/shard_map/ppermute | solution.py:149
  34.4 5.6 %collective-permute-start = (bf16[16,128,512]{2,1,0:T(8,128)(2,1)S(1)}, bf16[16,128,512]{2,1,0:T(8,128)(2,1)S(1)}, u32[]{:S(2)}, u32[]{:S(2)}) collective-permute-start(bf16[16,128,512]{2,1,0:T(8,128)(2,1)S(1)} %all_to_all.15.own), channel_id=1, source_target_pairs={{0,1},{1,2},{2,3},{3,4},{4,5},{5,6},{6,7},{7,8},{8,9},{9,10},{10,1... | collective-permute-start | bytes 6291464 | tf_op jit(solution)/shard_map/ppermute | solution.py:148
  40.0 21.8 %collective-permute-done.1.down = bf16[16,128,512]{2,1,0:T(8,128)(2,1)S(1)} collective-permute-done((bf16[16,128,512]{2,1,0:T(8,128)(2,1)S(1)}, bf16[16,128,512]{2,1,0:T(8,128)(2,1)S(1)}, u32[]{:S(2)}, u32[]{:S(2)}) %collective-permute-start.1) | collective-permute-done | bytes 2097184 | tf_op jit(solution)/shard_map/ppermute | solution.py:149
  61.8 1.2 %collective-permute-done.up = bf16[16,128,512]{2,1,0:T(8,128)(2,1)S(1)} collective-permute-done((bf16[16,128,512]{2,1,0:T(8,128)(2,1)S(1)}, bf16[16,128,512]{2,1,0:T(8,128)(2,1)S(1)}, u32[]{:S(2)}, u32[]{:S(2)}) %collective-permute-start) | collective-permute-done | bytes 2097184 | tf_op jit(solution)/shard_map/ppermute | solution.py:148
  62.9 0.0 copy-done
  62.9 0.0 copy-done.1
  62.9 2.4 %warp.1 = bf16[64,128,128]{2,1,0:T(8,128)(2,1)S(1)} custom-call(s32[64]{0:T(128)S(1)} %bitcast.14, s32[64]{0:T(128)S(1)} %bitcast.15, bf16[16,128,512]{2,1,0:T(8,128)(2,1)S(1)} %collective-permute-done.up, bf16[16,128,512]{2,1,0:T(8,128)(2,1)S(1)} %all_to_all.15.own, bf16[16,128,512]{2,1,0:T(8,128)(2,1)S(1)} %collective-permute-done.1.down), custom_call_target="tpu_custom_call" | custom-call | bytes 8388608 | tf_op jit(solution)/shard_map/warp/pallas_call | solution.py:32
  65.3 34.9 %all_to_all.16.blocks = bf16[8,8,128,128]{3,2,1,0:T(8,128)(2,1)S(1)} all-to-all(bf16[8,8,128,128]{3,2,1,0:T(8,128)(2,1)S(1)} %bitcast.13), channel_id=1, replica_groups=mesh['sec'=8,'row'=16] {'sec'}, dimensions={0} | all-to-all | bytes 4194304 | tf_op jit(solution)/shard_map/all_to_all | solution.py:152
  100.2 6.1 %scores.1 = f32[8,2,3,8,128]{4,3,2,1,0:T(8,128)S(1)} custom-call(bf16[8,8,128,128]{3,2,1,0:T(8,128)(2,1)S(1)} %all_to_all.16.blocks), custom_call_target="tpu_custom_call" | custom-call | flops 1207959552 | bytes 2097152 | tf_op jit(solution)/shard_map/scores/pallas_call | solution.py:118
  106.3 10.2 %all_to_all.17 = f32[8,2,3,8,128]{4,3,2,1,0:T(8,128)S(1)} all-to-all(f32[8,2,3,8,128]{4,3,2,1,0:T(8,128)S(1)} %scores.1), channel_id=1, replica_groups=mesh['sec'=8,'row'=16] {'sec'}, dimensions={0} | all-to-all | bytes 393216 | tf_op jit(solution)/shard_map/all_to_all | solution.py:154
  116.5 0.7 copy_bitcast_fusion
  (1 shorter events, 0.0 us)
Async XLA Ops:
  0.6 62.3 %copy-start = (s32[1,1,64]{2,1,0:T(1,128)S(1)}, s32[1,1,64]{2,1,0:T(1,128)}, u32[]{:S(2)}) copy-start(s32[1,1,64]{2,1,0:T(1,128)} %param.4) | copy-start | bytes 772
  0.6 62.3 %copy-start.1 = (s32[1,1,64]{2,1,0:T(1,128)S(1)}, s32[1,1,64]{2,1,0:T(1,128)}, u32[]{:S(2)}) copy-start(s32[1,1,64]{2,1,0:T(1,128)} %param.5) | copy-start | bytes 772
  32.3 29.5 %collective-permute-start.1 = (bf16[16,128,512]{2,1,0:T(8,128)(2,1)S(1)}, bf16[16,128,512]{2,1,0:T(8,128)(2,1)S(1)}, u32[]{:S(2)}, u32[]{:S(2)}) collective-permute-start(bf16[16,128,512]{2,1,0:T(8,128)(2,1)S(1)} %all_to_all.15.own), channel_id=1, source_target_pairs={{1,0},{2,1},{3,2},{4,3},{5,4},{6,5},{7,6},{8,7},{9,8},{10,9},{11,1... | collective-permute-start | bytes 6291464 | tf_op jit(solution)/shard_map/ppermute | solution.py:149
  34.4 28.5 %collective-permute-start = (bf16[16,128,512]{2,1,0:T(8,128)(2,1)S(1)}, bf16[16,128,512]{2,1,0:T(8,128)(2,1)S(1)}, u32[]{:S(2)}, u32[]{:S(2)}) collective-permute-start(bf16[16,128,512]{2,1,0:T(8,128)(2,1)S(1)} %all_to_all.15.own), channel_id=1, source_target_pairs={{0,1},{1,2},{2,3},{3,4},{4,5},{5,6},{6,7},{7,8},{8,9},{9,10},{10,1... | collective-permute-start | bytes 6291464 | tf_op jit(solution)/shard_map/ppermute | solution.py:148

commit v3 on v2

--- a/solution.py
+++ b/solution.py
@@ -11,23 +11,24 @@
 LAGS = 3
 
 
-def warp_kernel(shifts, columns, up, own, down, out):
+def warp_kernel(shifts, columns, own, beside, across, out):
     width = own.shape[2] // BLOCK
+    toward = 2 * lax.rem(lax.axis_index("row"), 2) - 1
 
     @pl.loop(0, out.shape[0], unroll=4)
     def _(j):
         column = columns[j]
         stripe = column // width
         lane = pl.multiple_of((column % width) * BLOCK, BLOCK)
-        shift = shifts[j]
-        for step, source in ((-1, up), (0, own), (1, down)):
+        side = shifts[j] * toward
+        for at, source in ((0, own), (-1, beside), (1, across)):
 
-            @pl.when(shift == step)
+            @pl.when(side == at)
             def _():
                 out[j] = source[stripe, :, pl.ds(lane, BLOCK)]
 
 
-def warp(shifts, columns, up, own, down):
+def warp(shifts, columns, own, beside, across):
     shape = (shifts.shape[0], BLOCK, BLOCK)
     return pl.pallas_call(
         warp_kernel,
@@ -40,7 +41,7 @@
             flops=0, bytes_accessed=8 * own.size, transcendentals=0
         ),
         name="warp",
-    )(shifts, columns, up, own, down)
+    )(shifts, columns, own, beside, across)
 
 
 def partial_lags(matrix):
@@ -140,14 +141,15 @@
     raw = raw_sections[0]
     rows = lax.axis_size("row")
     sections = lax.axis_size("sec")
-    stripes = lax.all_to_all(
-        raw.reshape(rows, -1, raw.shape[1]), "row", split_axis=0, concat_axis=0, tiled=True
+    own = lax.all_to_all(
+        raw.reshape(rows, BLOCK, raw.shape[1]), "row", split_axis=0, concat_axis=0, tiled=True
     )
-    forward = [(i, i + 1) for i in range(rows - 1)]
-    backward = [(target, source) for source, target in forward]
-    up = lax.ppermute(stripes, "row", forward)
-    down = lax.ppermute(stripes, "row", backward)
-    warped = warp(shift_rows[0, 0], source_cols[0, 0], up, stripes, down)
+    chips = rows // 2
+    links = [(2 * r, 2 * r - 1) for r in range(1, chips)]
+    links += [(2 * r + 1, 2 * r + 2) for r in range(chips - 1)]
+    across = lax.ppermute(own, "row", links)
+    beside = lax.ppermute(own, "row", [(i, i ^ 1) for i in range(rows)])
+    warped = warp(shift_rows[0, 0], source_cols[0, 0], own, beside, across)
     warped = warped.reshape(sections, -1, BLOCK, BLOCK)
     chunk = lax.all_to_all(warped, "sec", split_axis=0, concat_axis=0, tiled=True)
     result = scores(chunk)

time: 119 us -> 116 us (0.975); the launches traced: 117 us -> 116 us
  starting transfers between devices: 7.66 us -> 4.05 us
  waiting for transfers between devices: 23 us -> 25.4 us
    ppermute x2, starting transfers between devices: 7.66 us -> 4.05 us  [the longest x1 3.97 us: body(): across = lax.ppermute(own, 'row', links)]
    ppermute x2, waiting for transfers between devices: 23 us -> 25.4 us  [the longest x1 25.4 us: body(): across = lax.ppermute(own, 'row', links)]
  transfers between devices with their start and end apart: 2 -> 2, of which waited for: 2 -> 1; matrix products, arithmetic and copies ran while one was open for 0% -> 0% of each run, Pallas kernels for 0% -> 0%
where the time goes in v3:
time: 116 us
  blocking collectives  76.3 us (66%)
  waiting for transfers between devices  25.4 us (22%)
  Pallas kernels  8.52 us (7%)
  starting transfers between devices  4.05 us (3%)
    all_to_all x1, blocking collectives, body(): lax.all_to_all(warped, 'sec', split_axis=0, concat_axis=0, tiled=True)  34.5 us
    all_to_all x1, blocking collectives, body(): lax.all_to_all(raw.reshape(rows, BLOCK, raw.shape[1]), 'row', split_axis=...  31.7 us
    ppermute x1, waiting for transfers between devices, body(): across = lax.ppermute(own, 'row', links)  25.4 us
    all_to_all x1, blocking collectives, body(): lax.all_to_all(result, 'sec', split_axis=0, concat_axis=0, tiled=True)  10.2 us
    pallas_call x1, Pallas kernels, scores(): pl.pallas_call(score_kernel, grid=(columns,), in_specs=[pl.BlockSpec((sec...  6.11 us
    ppermute x1, starting transfers between devices, body(): across = lax.ppermute(own, 'row', links)  3.97 us
    pallas_call x1, Pallas kernels, warp(): pl.pallas_call(warp_kernel, in_specs=[pl.BlockSpec(memory_space=pltpu.SME...  2.41 us
  transfers between devices with their start and end apart: 2, of which 1 were waited for; matrix products, arithmetic and copies ran while one was open for 0% of the time, Pallas kernels for 0%

profile of v3, /device:TPU:25, one launch (start us, length us, event | category | flops | bytes accessed | tf_op | source)
XLA Modules:
  0.0 115.7 jit_solution(1698375515210386986)
XLA Ops:
  0.6 0.0 copy-start
  0.6 0.0 copy-start.1
  0.6 31.7 %all_to_all.15.own = bf16[16,128,512]{2,1,0:T(8,128)(2,1)S(1)} all-to-all(bf16[16,128,512]{2,1,0:T(8,128)(2,1)} %bitcast.16), channel_id=1, replica_groups=mesh['sec'=8,'row'=16] {'row'}, dimensions={0} | all-to-all | bytes 4194304 | tf_op jit(solution)/shard_map/all_to_all | solution.py:144
  32.3 4.0 %collective-permute-start.1 = (bf16[16,128,512]{2,1,0:T(8,128)(2,1)S(1)}, bf16[16,128,512]{2,1,0:T(8,128)(2,1)S(1)}, u32[]{:S(2)}, u32[]{:S(2)}) collective-permute-start(bf16[16,128,512]{2,1,0:T(8,128)(2,1)S(1)} %all_to_all.15.own), channel_id=1, source_target_pairs={{2,1},{4,3},{6,5},{8,7},{10,9},{12,11},{14,13},{1,2},{3,4},{5,6},{... | collective-permute-start | bytes 6291464 | tf_op jit(solution)/shard_map/ppermute | solution.py:150
  36.3 0.1 collective-permute-start
  36.4 25.4 %collective-permute-done.1.across = bf16[16,128,512]{2,1,0:T(8,128)(2,1)S(1)} collective-permute-done((bf16[16,128,512]{2,1,0:T(8,128)(2,1)S(1)}, bf16[16,128,512]{2,1,0:T(8,128)(2,1)S(1)}, u32[]{:S(2)}, u32[]{:S(2)}) %collective-permute-start.1) | collective-permute-done | bytes 2097184 | tf_op jit(solution)/shard_map/ppermute | solution.py:150
  61.8 0.0 collective-permute-done.beside
  61.8 0.0 copy-done
  61.8 0.0 copy-done.1
  61.8 2.4 %warp.1 = bf16[64,128,128]{2,1,0:T(8,128)(2,1)S(1)} custom-call(s32[64]{0:T(128)S(1)} %bitcast.14, s32[64]{0:T(128)S(1)} %bitcast.15, bf16[16,128,512]{2,1,0:T(8,128)(2,1)S(1)} %all_to_all.15.own, bf16[16,128,512]{2,1,0:T(8,128)(2,1)S(1)} %collective-permute-done.beside, bf16[16,128,512]{2,1,0:T(8,128)(2,1)S(1)} %collective-permute-done.1.across), custom_call_target="tpu_custom_call" | custom-call | bytes 8388608 | tf_op jit(solution)/shard_map/warp/pallas_call | solution.py:33
  64.2 34.5 %all_to_all.16.blocks = bf16[8,8,128,128]{3,2,1,0:T(8,128)(2,1)S(1)} all-to-all(bf16[8,8,128,128]{3,2,1,0:T(8,128)(2,1)S(1)} %bitcast.13), channel_id=1, replica_groups=mesh['sec'=8,'row'=16] {'sec'}, dimensions={0} | all-to-all | bytes 4194304 | tf_op jit(solution)/shard_map/all_to_all | solution.py:154
  98.7 6.1 %scores.1 = f32[8,2,3,8,128]{4,3,2,1,0:T(8,128)S(1)} custom-call(bf16[8,8,128,128]{3,2,1,0:T(8,128)(2,1)S(1)} %all_to_all.16.blocks), custom_call_target="tpu_custom_call" | custom-call | flops 1207959552 | bytes 2097152 | tf_op jit(solution)/shard_map/scores/pallas_call | solution.py:119
  104.8 10.2 %all_to_all.17 = f32[8,2,3,8,128]{4,3,2,1,0:T(8,128)S(1)} all-to-all(f32[8,2,3,8,128]{4,3,2,1,0:T(8,128)S(1)} %scores.1), channel_id=1, replica_groups=mesh['sec'=8,'row'=16] {'sec'}, dimensions={0} | all-to-all | bytes 393216 | tf_op jit(solution)/shard_map/all_to_all | solution.py:156
  115.0 0.7 copy_bitcast_fusion
  (1 shorter events, 0.0 us)
Async XLA Ops:
  0.6 61.1 %copy-start = (s32[1,1,64]{2,1,0:T(1,128)S(1)}, s32[1,1,64]{2,1,0:T(1,128)}, u32[]{:S(2)}) copy-start(s32[1,1,64]{2,1,0:T(1,128)} %param.4) | copy-start | bytes 772
  0.6 61.1 %copy-start.1 = (s32[1,1,64]{2,1,0:T(1,128)S(1)}, s32[1,1,64]{2,1,0:T(1,128)}, u32[]{:S(2)}) copy-start(s32[1,1,64]{2,1,0:T(1,128)} %param.5) | copy-start | bytes 772
  32.3 29.5 %collective-permute-start.1 = (bf16[16,128,512]{2,1,0:T(8,128)(2,1)S(1)}, bf16[16,128,512]{2,1,0:T(8,128)(2,1)S(1)}, u32[]{:S(2)}, u32[]{:S(2)}) collective-permute-start(bf16[16,128,512]{2,1,0:T(8,128)(2,1)S(1)} %all_to_all.15.own), channel_id=1, source_target_pairs={{2,1},{4,3},{6,5},{8,7},{10,9},{12,11},{14,13},{1,2},{3,4},{5,6},{... | collective-permute-start | bytes 6291464 | tf_op jit(solution)/shard_map/ppermute | solution.py:150
  36.3 25.5 %collective-permute-start = (bf16[16,128,512]{2,1,0:T(8,128)(2,1)S(1)}, bf16[16,128,512]{2,1,0:T(8,128)(2,1)S(1)}, u32[]{:S(2)}, u32[]{:S(2)}) collective-permute-start(bf16[16,128,512]{2,1,0:T(8,128)(2,1)S(1)} %all_to_all.15.own), channel_id=1, source_target_pairs={{0,1},{1,0},{2,3},{3,2},{4,5},{5,4},{6,7},{7,6},{8,9},{9,8},{10,11... | collective-permute-start | bytes 6291464 | tf_op jit(solution)/shard_map/ppermute | solution.py:151

commit v4 on v3

--- a/solution.py
+++ b/solution.py
@@ -9,23 +9,23 @@
 
 BLOCK = 128
 LAGS = 3
+GROUP = 2
 
 
 def warp_kernel(shifts, columns, own, beside, across, out):
     width = own.shape[2] // BLOCK
     toward = 2 * lax.rem(lax.axis_index("row"), 2) - 1
 
-    @pl.loop(0, out.shape[0], unroll=4)
+    @pl.loop(0, out.shape[0], unroll=8)
     def _(j):
         column = columns[j]
-        stripe = column // width
-        lane = pl.multiple_of((column % width) * BLOCK, BLOCK)
+        stripe = lax.div(column, width)
+        lane = pl.multiple_of(lax.rem(column, width) * BLOCK, BLOCK)
         side = shifts[j] * toward
-        for at, source in ((0, own), (-1, beside), (1, across)):
-
-            @pl.when(side == at)
-            def _():
-                out[j] = source[stripe, :, pl.ds(lane, BLOCK)]
+        here = own[stripe, :, pl.ds(lane, BLOCK)]
+        low = beside[stripe, :, pl.ds(lane, BLOCK)]
+        high = across[stripe, :, pl.ds(lane, BLOCK)]
+        out[j] = jnp.where(side == 0, here, jnp.where(side == 1, high, low))
 
 
 def warp(shifts, columns, own, beside, across):
@@ -59,37 +59,41 @@
     return jnp.concatenate([block[BLOCK // 2 :], block[: BLOCK // 2]], axis=0)
 
 
-def score_kernel(blocks, out, flipped, by_row, by_column, lags, squares):
-    sections = blocks.shape[0]
+def score_kernel(blocks, out, flipped, by_column, lags, squares):
+    sections, group = blocks.shape[:2]
     steps = out.shape[3]
-    place = pl.ds(pl.multiple_of(pl.program_id(0) * 8, 8), 8)
-    for s in range(sections):
-        block = blocks[s, 0]
-        flip = block.T
-        flipped[s] = flip
-        by_row[s, :BLOCK] = flip
-        by_row[s, BLOCK:] = turned(block).T
-        by_column[s, :BLOCK] = block
-        by_column[s, BLOCK:] = pltpu.roll(block, BLOCK // 2, axis=1)
-        values = block.astype(jnp.float32)
-        values = values * values
-        total = values[0:8]
-        for start in range(8, BLOCK, 8):
-            total = total + values[start : start + 8]
-        squares[s, place, :] = total
-    for back in range(sections - 1):
-        count = min(LAGS, sections - 1 - back)
-        near = range(back + 1, back + 1 + count)
-        current = jnp.concatenate([halves(blocks[s, 0]) for s in near], axis=0)
-        current_flipped = jnp.concatenate([halves(flipped[s]) for s in near], axis=0)
-        row_corr = jnp.dot(current, by_row[back], preferred_element_type=jnp.float32)
-        col_corr = jnp.dot(current_flipped, by_column[back], preferred_element_type=jnp.float32)
-        for k in range(count):
-            part = slice(k * BLOCK // 2, (k + 1) * BLOCK // 2)
-            lags[back + 1 + k, 0, k, place, :] = partial_lags(row_corr[part])
-            lags[back + 1 + k, 1, k, place, :] = partial_lags(col_corr[part])
+    for column in range(group):
+        place = pl.ds(pl.multiple_of((pl.program_id(0) * group + column) * 8, 8), 8)
+        by_row = []
+        for s in range(sections):
+            block = blocks[s, column]
+            by_row.append(jnp.concatenate([block, turned(block)], axis=1))
+            flipped[s] = block.T
+            by_column[s, :BLOCK] = block
+            by_column[s, BLOCK:] = pltpu.roll(block, BLOCK // 2, axis=1)
+            values = block.astype(jnp.float32)
+            values = values * values
+            total = values[0:8]
+            for start in range(8, BLOCK, 8):
+                total = total + values[start : start + 8]
+            squares[s, place, :] = total
+        for back in range(sections - 1):
+            count = min(LAGS, sections - 1 - back)
+            near = range(back + 1, back + 1 + count)
+            current = jnp.concatenate([halves(blocks[s, column]) for s in near], axis=0)
+            current_flipped = jnp.concatenate([halves(flipped[s]) for s in near], axis=0)
+            row_corr = lax.dot_general(
+                current, by_row[back], (((1,), (1,)), ((), ())), preferred_element_type=jnp.float32
+            )
+            col_corr = jnp.dot(
+                current_flipped, by_column[back], preferred_element_type=jnp.float32
+            )
+            for k in range(count):
+                part = slice(k * BLOCK // 2, (k + 1) * BLOCK // 2)
+                lags[back + 1 + k, 0, k, place, :] = partial_lags(row_corr[part])
+                lags[back + 1 + k, 1, k, place, :] = partial_lags(col_corr[part])
 
-    @pl.when(pl.program_id(0) == steps - 1)
+    @pl.when(pl.program_id(0) == pl.num_programs(0) - 1)
     def _():
         energies = []
         for s in range(sections):
@@ -118,13 +122,12 @@
     pairs = LAGS * sections - LAGS * (LAGS + 1) // 2
     return pl.pallas_call(
         score_kernel,
-        grid=(columns,),
-        in_specs=[pl.BlockSpec((sections, 1, BLOCK, BLOCK), lambda j: (0, j, 0, 0))],
+        grid=(columns // GROUP,),
+        in_specs=[pl.BlockSpec((sections, GROUP, BLOCK, BLOCK), lambda j: (0, j, 0, 0))],
         out_specs=pl.BlockSpec(shape, lambda j: (0, 0, 0, 0, 0)),
         out_shape=jax.ShapeDtypeStruct(shape, jnp.float32),
         scratch_shapes=[
             pltpu.VMEM((sections, BLOCK, BLOCK), jnp.bfloat16),
-            pltpu.VMEM((sections, 2 * BLOCK, BLOCK), jnp.bfloat16),
             pltpu.VMEM((sections, 2 * BLOCK, BLOCK), jnp.bfloat16),
             pltpu.VMEM((sections, 2, LAGS, columns * 8, BLOCK), jnp.float32),
             pltpu.VMEM((sections, columns * 8, BLOCK), jnp.float32),

time: 116 us -> 114 us (0.983)
  Pallas kernels: 8.52 us -> 6.55 us
where the time goes in v4:
time: 114 us
  blocking collectives  76.3 us (67%)
  waiting for transfers between devices  25.4 us (22%)
  Pallas kernels  6.55 us (6%)
  starting transfers between devices  4.05 us (4%)
    all_to_all x1, blocking collectives, body(): lax.all_to_all(warped, 'sec', split_axis=0, concat_axis=0, tiled=True)  34.5 us
    all_to_all x1, blocking collectives, body(): lax.all_to_all(raw.reshape(rows, BLOCK, raw.shape[1]), 'row', split_axis=...  31.7 us
    ppermute x1, waiting for transfers between devices, body(): across = lax.ppermute(own, 'row', links)  25.4 us
    all_to_all x1, blocking collectives, body(): lax.all_to_all(result, 'sec', split_axis=0, concat_axis=0, tiled=True)  10.2 us
    pallas_call x1, Pallas kernels, scores(): pl.pallas_call(score_kernel, grid=(columns // GROUP,), in_specs=[pl.Block...  5.05 us
    ppermute x1, starting transfers between devices, body(): across = lax.ppermute(own, 'row', links)  3.97 us
  transfers between devices with their start and end apart: 2, of which 1 were waited for; matrix products, arithmetic and copies ran while one was open for 0% of the time, Pallas kernels for 0%

profile of v4, /device:TPU:25, one launch (start us, length us, event | category | flops | bytes accessed | tf_op | source)
XLA Modules:
  0.0 113.7 jit_solution(15020080858200174564)
XLA Ops:
  0.6 0.0 copy-start
  0.6 0.0 copy-start.1
  0.6 31.7 %all_to_all.15.own = bf16[16,128,512]{2,1,0:T(8,128)(2,1)S(1)} all-to-all(bf16[16,128,512]{2,1,0:T(8,128)(2,1)} %bitcast.16), channel_id=1, replica_groups=mesh['sec'=8,'row'=16] {'row'}, dimensions={0} | all-to-all | bytes 4194304 | tf_op jit(solution)/shard_map/all_to_all | solution.py:147
  32.3 4.0 %collective-permute-start.1 = (bf16[16,128,512]{2,1,0:T(8,128)(2,1)S(1)}, bf16[16,128,512]{2,1,0:T(8,128)(2,1)S(1)}, u32[]{:S(2)}, u32[]{:S(2)}) collective-permute-start(bf16[16,128,512]{2,1,0:T(8,128)(2,1)S(1)} %all_to_all.15.own), channel_id=1, source_target_pairs={{2,1},{4,3},{6,5},{8,7},{10,9},{12,11},{14,13},{1,2},{3,4},{5,6},{... | collective-permute-start | bytes 6291464 | tf_op jit(solution)/shard_map/ppermute | solution.py:153
  36.3 0.1 collective-permute-start
  36.4 25.4 %collective-permute-done.1.across = bf16[16,128,512]{2,1,0:T(8,128)(2,1)S(1)} collective-permute-done((bf16[16,128,512]{2,1,0:T(8,128)(2,1)S(1)}, bf16[16,128,512]{2,1,0:T(8,128)(2,1)S(1)}, u32[]{:S(2)}, u32[]{:S(2)}) %collective-permute-start.1) | collective-permute-done | bytes 2097184 | tf_op jit(solution)/shard_map/ppermute | solution.py:153
  61.8 0.0 collective-permute-done.beside
  61.8 0.0 copy-done
  61.8 0.0 copy-done.1
  61.8 1.5 %warp.1 = bf16[64,128,128]{2,1,0:T(8,128)(2,1)S(1)} custom-call(s32[64]{0:T(128)S(1)} %bitcast.14, s32[64]{0:T(128)S(1)} %bitcast.15, bf16[16,128,512]{2,1,0:T(8,128)(2,1)S(1)} %all_to_all.15.own, bf16[16,128,512]{2,1,0:T(8,128)(2,1)S(1)} %collective-permute-done.beside, bf16[16,128,512]{2,1,0:T(8,128)(2,1)S(1)} %collective-permute-done.1.across), custom_call_target="tpu_custom_call" | custom-call | bytes 8388608 | tf_op jit(solution)/shard_map/warp/pallas_call | solution.py:33
  63.3 34.5 %all_to_all.16.blocks = bf16[8,8,128,128]{3,2,1,0:T(8,128)(2,1)S(1)} all-to-all(bf16[8,8,128,128]{3,2,1,0:T(8,128)(2,1)S(1)} %bitcast.13), channel_id=1, replica_groups=mesh['sec'=8,'row'=16] {'sec'}, dimensions={0} | all-to-all | bytes 4194304 | tf_op jit(solution)/shard_map/all_to_all | solution.py:157
  97.8 5.1 %scores.1 = f32[8,2,3,8,128]{4,3,2,1,0:T(8,128)S(1)} custom-call(bf16[8,8,128,128]{3,2,1,0:T(8,128)(2,1)S(1)} %all_to_all.16.blocks), custom_call_target="tpu_custom_call" | custom-call | flops 1207959552 | bytes 2097152 | tf_op jit(solution)/shard_map/scores/pallas_call | solution.py:123
  102.8 10.2 %all_to_all.17 = f32[8,2,3,8,128]{4,3,2,1,0:T(8,128)S(1)} all-to-all(f32[8,2,3,8,128]{4,3,2,1,0:T(8,128)S(1)} %scores.1), channel_id=1, replica_groups=mesh['sec'=8,'row'=16] {'sec'}, dimensions={0} | all-to-all | bytes 393216 | tf_op jit(solution)/shard_map/all_to_all | solution.py:159
  113.0 0.7 copy_bitcast_fusion
  (1 shorter events, 0.0 us)
Async XLA Ops:
  0.6 61.1 %copy-start = (s32[1,1,64]{2,1,0:T(1,128)S(1)}, s32[1,1,64]{2,1,0:T(1,128)}, u32[]{:S(2)}) copy-start(s32[1,1,64]{2,1,0:T(1,128)} %param.4) | copy-start | bytes 772
  0.6 61.1 %copy-start.1 = (s32[1,1,64]{2,1,0:T(1,128)S(1)}, s32[1,1,64]{2,1,0:T(1,128)}, u32[]{:S(2)}) copy-start(s32[1,1,64]{2,1,0:T(1,128)} %param.5) | copy-start | bytes 772
  32.3 29.5 %collective-permute-start.1 = (bf16[16,128,512]{2,1,0:T(8,128)(2,1)S(1)}, bf16[16,128,512]{2,1,0:T(8,128)(2,1)S(1)}, u32[]{:S(2)}, u32[]{:S(2)}) collective-permute-start(bf16[16,128,512]{2,1,0:T(8,128)(2,1)S(1)} %all_to_all.15.own), channel_id=1, source_target_pairs={{2,1},{4,3},{6,5},{8,7},{10,9},{12,11},{14,13},{1,2},{3,4},{5,6},{... | collective-permute-start | bytes 6291464 | tf_op jit(solution)/shard_map/ppermute | solution.py:153
  36.3 25.5 %collective-permute-start = (bf16[16,128,512]{2,1,0:T(8,128)(2,1)S(1)}, bf16[16,128,512]{2,1,0:T(8,128)(2,1)S(1)}, u32[]{:S(2)}, u32[]{:S(2)}) collective-permute-start(bf16[16,128,512]{2,1,0:T(8,128)(2,1)S(1)} %all_to_all.15.own), channel_id=1, source_target_pairs={{0,1},{1,0},{2,3},{3,2},{4,5},{5,4},{6,7},{7,6},{8,9},{9,8},{10,11... | collective-permute-start | bytes 6291464 | tf_op jit(solution)/shard_map/ppermute | solution.py:154

commit v5 on v4

--- a/solution.py
+++ b/solution.py
@@ -9,7 +9,6 @@
 
 BLOCK = 128
 LAGS = 3
-GROUP = 2
 
 
 def warp_kernel(shifts, columns, own, beside, across, out):
@@ -56,21 +55,24 @@
 
 
 def turned(block):
-    return jnp.concatenate([block[BLOCK // 2 :], block[: BLOCK // 2]], axis=0)
+    half = BLOCK // 2
+    return jnp.concatenate([block, jnp.concatenate([block[half:], block[:half]], axis=0)], axis=1)
 
 
-def score_kernel(blocks, out, flipped, by_column, lags, squares):
-    sections, group = blocks.shape[:2]
-    steps = out.shape[3]
-    for column in range(group):
-        place = pl.ds(pl.multiple_of((pl.program_id(0) * group + column) * 8, 8), 8)
-        by_row = []
+def along_lanes(left, right):
+    return lax.dot_general(
+        left, right, (((1,), (1,)), ((), ())), preferred_element_type=jnp.float32
+    )
+
+
+def score_kernel(blocks, out, flipped, lags, squares):
+    sections, columns = blocks.shape[:2]
+    half = BLOCK // 2
+    for column in range(columns):
+        place = slice(column * 8, (column + 1) * 8)
         for s in range(sections):
             block = blocks[s, column]
-            by_row.append(jnp.concatenate([block, turned(block)], axis=1))
             flipped[s] = block.T
-            by_column[s, :BLOCK] = block
-            by_column[s, BLOCK:] = pltpu.roll(block, BLOCK // 2, axis=1)
             values = block.astype(jnp.float32)
             values = values * values
             total = values[0:8]
@@ -82,38 +84,31 @@
             near = range(back + 1, back + 1 + count)
             current = jnp.concatenate([halves(blocks[s, column]) for s in near], axis=0)
             current_flipped = jnp.concatenate([halves(flipped[s]) for s in near], axis=0)
-            row_corr = lax.dot_general(
-                current, by_row[back], (((1,), (1,)), ((), ())), preferred_element_type=jnp.float32
-            )
-            col_corr = jnp.dot(
-                current_flipped, by_column[back], preferred_element_type=jnp.float32
-            )
+            row_corr = along_lanes(current, turned(blocks[back, column]))
+            col_corr = along_lanes(current_flipped, turned(flipped[back]))
             for k in range(count):
-                part = slice(k * BLOCK // 2, (k + 1) * BLOCK // 2)
+                part = slice(k * half, (k + 1) * half)
                 lags[back + 1 + k, 0, k, place, :] = partial_lags(row_corr[part])
                 lags[back + 1 + k, 1, k, place, :] = partial_lags(col_corr[part])
-
-    @pl.when(pl.program_id(0) == pl.num_programs(0) - 1)
-    def _():
-        energies = []
-        for s in range(sections):
-            total = squares[s, pl.ds(0, steps, stride=8), :]
-            for b in range(1, 8):
-                total = total + squares[s, pl.ds(b, steps, stride=8), :]
-            energies.append(jnp.sum(total, axis=1, keepdims=True) / (BLOCK * BLOCK))
-        for s in range(sections):
-            for k in range(1, LAGS + 1):
-                if s < k:
-                    for way in range(2):
-                        out[s, way, k - 1] = jnp.zeros((steps, BLOCK), jnp.float32)
-                    continue
-                scaling = 1.0 / (BLOCK * jnp.sqrt(energies[s] * energies[s - k] + 1e-06))
+    energies = []
+    for s in range(sections):
+        total = squares[s, pl.ds(0, columns, stride=8), :]
+        for b in range(1, 8):
+            total = total + squares[s, pl.ds(b, columns, stride=8), :]
+        energies.append(jnp.sum(total, axis=1, keepdims=True) / (BLOCK * BLOCK))
+    for s in range(sections):
+        for k in range(1, LAGS + 1):
+            if s < k:
                 for way in range(2):
-                    total = lags[s, way, k - 1, pl.ds(0, steps, stride=8), :]
-                    for b in range(1, 8):
-                        row = lags[s, way, k - 1, pl.ds(b, steps, stride=8), :]
-                        total = total + pltpu.roll(row, BLOCK - b, axis=1)
-                    out[s, way, k - 1] = total * scaling
+                    out[s, way, k - 1] = jnp.zeros((columns, BLOCK), jnp.float32)
+                continue
+            scaling = 1.0 / (BLOCK * jnp.sqrt(energies[s] * energies[s - k] + 1e-06))
+            for way in range(2):
+                total = lags[s, way, k - 1, pl.ds(0, columns, stride=8), :]
+                for b in range(1, 8):
+                    row = lags[s, way, k - 1, pl.ds(b, columns, stride=8), :]
+                    total = total + pltpu.roll(row, BLOCK - b, axis=1)
+                out[s, way, k - 1] = total * scaling
 
 
 def scores(blocks):
@@ -122,13 +117,11 @@
     pairs = LAGS * sections - LAGS * (LAGS + 1) // 2
     return pl.pallas_call(
         score_kernel,
-        grid=(columns // GROUP,),
-        in_specs=[pl.BlockSpec((sections, GROUP, BLOCK, BLOCK), lambda j: (0, j, 0, 0))],
-        out_specs=pl.BlockSpec(shape, lambda j: (0, 0, 0, 0, 0)),
+        in_specs=[pl.BlockSpec(memory_space=pltpu.VMEM)],
+        out_specs=pl.BlockSpec(memory_space=pltpu.VMEM),
         out_shape=jax.ShapeDtypeStruct(shape, jnp.float32),
         scratch_shapes=[
             pltpu.VMEM((sections, BLOCK, BLOCK), jnp.bfloat16),
-            pltpu.VMEM((sections, 2 * BLOCK, BLOCK), jnp.bfloat16),
             pltpu.VMEM((sections, 2, LAGS, columns * 8, BLOCK), jnp.float32),
             pltpu.VMEM((sections, columns * 8, BLOCK), jnp.float32),
         ],

time: 114 us -> 113 us (level)
  Pallas kernels: 6.55 us -> 4.8 us
    pallas_call x1, Pallas kernels: 5.05 us -> 3.3 us  [scores(): pl.pallas_call(score_kernel, in_specs=[pl.BlockSpec(memory_space=pltpu.VM...]
where the time goes in v5:
time: 113 us; the launch traced here: 112 us
  blocking collectives  76.4 us (68%)
  waiting for transfers between devices  25.4 us (22%)
  Pallas kernels  4.8 us (4%)
  starting transfers between devices  4.05 us (4%)
    all_to_all x1, blocking collectives, body(): lax.all_to_all(warped, 'sec', split_axis=0, concat_axis=0, tiled=True)  34.5 us
    all_to_all x1, blocking collectives, body(): lax.all_to_all(raw.reshape(rows, BLOCK, raw.shape[1]), 'row', split_axis=...  31.7 us
    ppermute x1, waiting for transfers between devices, body(): across = lax.ppermute(own, 'row', links)  25.4 us
    all_to_all x1, blocking collectives, body(): lax.all_to_all(result, 'sec', split_axis=0, concat_axis=0, tiled=True)  10.2 us
    ppermute x1, starting transfers between devices, body(): across = lax.ppermute(own, 'row', links)  3.97 us
    pallas_call x1, Pallas kernels, scores(): pl.pallas_call(score_kernel, in_specs=[pl.BlockSpec(memory_space=pltpu.VM...  3.3 us
  transfers between devices with their start and end apart: 2, of which 1 were waited for; matrix products, arithmetic and copies ran while one was open for 0% of the time, Pallas kernels for 0%

profile of v5, /device:TPU:25, one launch (start us, length us, event | category | flops | bytes accessed | tf_op | source)
XLA Modules:
  0.0 112.0 jit_solution(7887346869814797685)
XLA Ops:
  0.6 0.0 copy-start
  0.6 0.0 copy-start.1
  0.6 31.7 %all_to_all.15.own = bf16[16,128,512]{2,1,0:T(8,128)(2,1)S(1)} all-to-all(bf16[16,128,512]{2,1,0:T(8,128)(2,1)} %bitcast.16), channel_id=1, replica_groups=mesh['sec'=8,'row'=16] {'row'}, dimensions={0} | all-to-all | bytes 4194304 | tf_op jit(solution)/shard_map/all_to_all | solution.py:140
  32.3 4.0 %collective-permute-start.1 = (bf16[16,128,512]{2,1,0:T(8,128)(2,1)S(1)}, bf16[16,128,512]{2,1,0:T(8,128)(2,1)S(1)}, u32[]{:S(2)}, u32[]{:S(2)}) collective-permute-start(bf16[16,128,512]{2,1,0:T(8,128)(2,1)S(1)} %all_to_all.15.own), channel_id=1, source_target_pairs={{2,1},{4,3},{6,5},{8,7},{10,9},{12,11},{14,13},{1,2},{3,4},{5,6},{... | collective-permute-start | bytes 6291464 | tf_op jit(solution)/shard_map/ppermute | solution.py:146
  36.3 0.1 collective-permute-start
  36.4 25.4 %collective-permute-done.1.across = bf16[16,128,512]{2,1,0:T(8,128)(2,1)S(1)} collective-permute-done((bf16[16,128,512]{2,1,0:T(8,128)(2,1)S(1)}, bf16[16,128,512]{2,1,0:T(8,128)(2,1)S(1)}, u32[]{:S(2)}, u32[]{:S(2)}) %collective-permute-start.1) | collective-permute-done | bytes 2097184 | tf_op jit(solution)/shard_map/ppermute | solution.py:146
  61.8 0.0 collective-permute-done.beside
  61.8 0.0 copy-done
  61.8 0.0 copy-done.1
  61.8 1.5 %warp.1 = bf16[64,128,128]{2,1,0:T(8,128)(2,1)S(1)} custom-call(s32[64]{0:T(128)S(1)} %bitcast.14, s32[64]{0:T(128)S(1)} %bitcast.15, bf16[16,128,512]{2,1,0:T(8,128)(2,1)S(1)} %all_to_all.15.own, bf16[16,128,512]{2,1,0:T(8,128)(2,1)S(1)} %collective-permute-done.beside, bf16[16,128,512]{2,1,0:T(8,128)(2,1)S(1)} %collective-permute-done.1.across), custom_call_target="tpu_custom_call" | custom-call | bytes 8388608 | tf_op jit(solution)/shard_map/warp/pallas_call | solution.py:32
  63.3 34.5 %all_to_all.16.blocks = bf16[8,8,128,128]{3,2,1,0:T(8,128)(2,1)S(1)} all-to-all(bf16[8,8,128,128]{3,2,1,0:T(8,128)(2,1)S(1)} %bitcast.13), channel_id=1, replica_groups=mesh['sec'=8,'row'=16] {'sec'}, dimensions={0} | all-to-all | bytes 4194304 | tf_op jit(solution)/shard_map/all_to_all | solution.py:150
  97.8 3.3 %scores.1 = f32[8,2,3,8,128]{4,3,2,1,0:T(8,128)S(1)} custom-call(bf16[8,8,128,128]{3,2,1,0:T(8,128)(2,1)S(1)} %all_to_all.16.blocks), custom_call_target="tpu_custom_call" | custom-call | flops 1207959552 | bytes 2097152 | tf_op jit(solution)/shard_map/scores/pallas_call | solution.py:118
  101.1 10.2 %all_to_all.17 = f32[8,2,3,8,128]{4,3,2,1,0:T(8,128)S(1)} all-to-all(f32[8,2,3,8,128]{4,3,2,1,0:T(8,128)S(1)} %scores.1), channel_id=1, replica_groups=mesh['sec'=8,'row'=16] {'sec'}, dimensions={0} | all-to-all | bytes 393216 | tf_op jit(solution)/shard_map/all_to_all | solution.py:152
  111.3 0.7 copy_bitcast_fusion
  (1 shorter events, 0.0 us)
Async XLA Ops:
  0.6 61.1 %copy-start = (s32[1,1,64]{2,1,0:T(1,128)S(1)}, s32[1,1,64]{2,1,0:T(1,128)}, u32[]{:S(2)}) copy-start(s32[1,1,64]{2,1,0:T(1,128)} %param.4) | copy-start | bytes 772
  0.6 61.1 %copy-start.1 = (s32[1,1,64]{2,1,0:T(1,128)S(1)}, s32[1,1,64]{2,1,0:T(1,128)}, u32[]{:S(2)}) copy-start(s32[1,1,64]{2,1,0:T(1,128)} %param.5) | copy-start | bytes 772
  32.3 29.5 %collective-permute-start.1 = (bf16[16,128,512]{2,1,0:T(8,128)(2,1)S(1)}, bf16[16,128,512]{2,1,0:T(8,128)(2,1)S(1)}, u32[]{:S(2)}, u32[]{:S(2)}) collective-permute-start(bf16[16,128,512]{2,1,0:T(8,128)(2,1)S(1)} %all_to_all.15.own), channel_id=1, source_target_pairs={{2,1},{4,3},{6,5},{8,7},{10,9},{12,11},{14,13},{1,2},{3,4},{5,6},{... | collective-permute-start | bytes 6291464 | tf_op jit(solution)/shard_map/ppermute | solution.py:146
  36.3 25.5 %collective-permute-start = (bf16[16,128,512]{2,1,0:T(8,128)(2,1)S(1)}, bf16[16,128,512]{2,1,0:T(8,128)(2,1)S(1)}, u32[]{:S(2)}, u32[]{:S(2)}) collective-permute-start(bf16[16,128,512]{2,1,0:T(8,128)(2,1)S(1)} %all_to_all.15.own), channel_id=1, source_target_pairs={{0,1},{1,0},{2,3},{3,2},{4,5},{5,4},{6,7},{7,6},{8,9},{9,8},{10,11... | collective-permute-start | bytes 6291464 | tf_op jit(solution)/shard_map/ppermute | solution.py:147

commit v6 on v5

--- a/solution.py
+++ b/solution.py
@@ -9,35 +9,39 @@
 
 BLOCK = 128
 LAGS = 3
+FIRST = 32
 
 
-def warp_kernel(shifts, columns, own, beside, across, out):
+def warp_kernel(shifts, columns, own, beside, across, *outs, first):
     width = own.shape[2] // BLOCK
     toward = 2 * lax.rem(lax.axis_index("row"), 2) - 1
+    rows = slice(first, first + across.shape[1])
+    for away, out in enumerate(outs):
+        begin = (lax.axis_index("sec") ^ away) * out.shape[0] if len(outs) > 1 else 0
 
-    @pl.loop(0, out.shape[0], unroll=8)
-    def _(j):
-        column = columns[j]
-        stripe = lax.div(column, width)
-        lane = pl.multiple_of(lax.rem(column, width) * BLOCK, BLOCK)
-        side = shifts[j] * toward
-        here = own[stripe, :, pl.ds(lane, BLOCK)]
-        low = beside[stripe, :, pl.ds(lane, BLOCK)]
-        high = across[stripe, :, pl.ds(lane, BLOCK)]
-        out[j] = jnp.where(side == 0, here, jnp.where(side == 1, high, low))
+        @pl.loop(0, out.shape[0], unroll=8)
+        def _(near):
+            column = columns[begin + near]
+            stripe = lax.div(column, width)
+            lane = pl.multiple_of(lax.rem(column, width) * BLOCK, BLOCK)
+            side = shifts[begin + near] * toward
+            here = own[stripe, rows, pl.ds(lane, BLOCK)]
+            low = beside[stripe, rows, pl.ds(lane, BLOCK)]
+            high = across[stripe, :, pl.ds(lane, BLOCK)]
+            out[near] = jnp.where(side == 0, here, jnp.where(side == 1, high, low))
 
 
-def warp(shifts, columns, own, beside, across):
-    shape = (shifts.shape[0], BLOCK, BLOCK)
+def warp(shifts, columns, own, beside, across, first, pieces, flops):
+    shape = (shifts.shape[0] // pieces, across.shape[1], BLOCK)
     return pl.pallas_call(
-        warp_kernel,
+        functools.partial(warp_kernel, first=first),
         in_specs=[pl.BlockSpec(memory_space=pltpu.SMEM)] * 2
         + [pl.BlockSpec(memory_space=pltpu.VMEM)] * 3,
-        out_specs=pl.BlockSpec(memory_space=pltpu.VMEM),
-        out_shape=jax.ShapeDtypeStruct(shape, jnp.bfloat16),
+        out_specs=[pl.BlockSpec(memory_space=pltpu.VMEM)] * pieces,
+        out_shape=[jax.ShapeDtypeStruct(shape, jnp.bfloat16)] * pieces,
         compiler_params=pltpu.CompilerParams(vmem_limit_bytes=16 * 1024 * 1024),
         cost_estimate=pl.CostEstimate(
-            flops=0, bytes_accessed=8 * own.size, transcendentals=0
+            flops=flops, bytes_accessed=8 * across.size, transcendentals=0
         ),
         name="warp",
     )(shifts, columns, own, beside, across)
@@ -65,9 +69,16 @@
     )
 
 
-def score_kernel(blocks, out, flipped, lags, squares):
-    sections, columns = blocks.shape[:2]
+def score_kernel(high, *refs):
+    sections, columns, rest = high.shape[:3]
+    lows, refs = refs[:sections], refs[sections:]
+    out, blocks, flipped, lags, squares = refs
+    cut = BLOCK - rest
     half = BLOCK // 2
+    me = lax.axis_index("sec")
+    for away, low in enumerate(lows):
+        blocks[me ^ away, :, :cut] = low[...]
+    blocks[:, :, cut:] = high[...]
     for column in range(columns):
         place = slice(column * 8, (column + 1) * 8)
         for s in range(sections):
@@ -111,26 +122,27 @@
                 out[s, way, k - 1] = total * scaling
 
 
-def scores(blocks):
-    sections, columns = blocks.shape[:2]
+def scores(lows, high):
+    sections, columns = high.shape[:2]
     shape = (sections, 2, LAGS, columns, BLOCK)
     pairs = LAGS * sections - LAGS * (LAGS + 1) // 2
     return pl.pallas_call(
         score_kernel,
-        in_specs=[pl.BlockSpec(memory_space=pltpu.VMEM)],
+        in_specs=[pl.BlockSpec(memory_space=pltpu.VMEM)] * (1 + sections),
         out_specs=pl.BlockSpec(memory_space=pltpu.VMEM),
         out_shape=jax.ShapeDtypeStruct(shape, jnp.float32),
         scratch_shapes=[
+            pltpu.VMEM((sections, columns, BLOCK, BLOCK), jnp.bfloat16),
             pltpu.VMEM((sections, BLOCK, BLOCK), jnp.bfloat16),
             pltpu.VMEM((sections, 2, LAGS, columns * 8, BLOCK), jnp.float32),
             pltpu.VMEM((sections, columns * 8, BLOCK), jnp.float32),
         ],
         compiler_params=pltpu.CompilerParams(vmem_limit_bytes=16 * 1024 * 1024),
         cost_estimate=pl.CostEstimate(
-            flops=4 * columns * pairs * BLOCK**3, bytes_accessed=2 * blocks.size, transcendentals=0
+            flops=4 * columns * pairs * BLOCK**3, bytes_accessed=4 * high.size, transcendentals=0
         ),
         name="scores",
-    )(blocks)
+    )(high, *lows)
 
 
 def body(raw_sections, shift_rows, source_cols):
@@ -143,12 +155,21 @@
     chips = rows // 2
     links = [(2 * r, 2 * r - 1) for r in range(1, chips)]
     links += [(2 * r + 1, 2 * r + 2) for r in range(chips - 1)]
-    across = lax.ppermute(own, "row", links)
+    shifts, columns = shift_rows[0, 0], source_cols[0, 0]
+    near = lax.ppermute(own[:, :FIRST], "row", links)
+    far = lax.ppermute(own[:, FIRST:], "row", links)
     beside = lax.ppermute(own, "row", [(i, i ^ 1) for i in range(rows)])
-    warped = warp(shift_rows[0, 0], source_cols[0, 0], own, beside, across)
-    warped = warped.reshape(sections, -1, BLOCK, BLOCK)
-    chunk = lax.all_to_all(warped, "sec", split_axis=0, concat_axis=0, tiled=True)
-    result = scores(chunk)
+
+    lows = warp(shifts, columns, own, beside, near, 0, sections, 12000000000)
+    lows = [
+        part if away == 0 else lax.ppermute(part, "sec", [(i, i ^ away) for i in range(sections)])
+        for away, part in enumerate(lows)
+    ]
+    shifts, lows = lax.optimization_barrier((shifts, lows))
+    (high,) = warp(shifts, columns, own, beside, far, FIRST, 1, 0)
+    high = high.reshape(sections, -1, BLOCK - FIRST, BLOCK)
+    high = lax.all_to_all(high, "sec", split_axis=0, concat_axis=0, tiled=True)
+    result = scores(lows, high)
     result = lax.all_to_all(result, "sec", split_axis=0, concat_axis=0, tiled=True)
     result = result.transpose(1, 2, 0, 3, 4).reshape(2, 1, LAGS, 1, -1, BLOCK)
     return result[0], result[1]

time: 113 us -> 111 us (0.982)
  starting transfers between devices: 4.05 us -> 21.9 us
  blocking collectives: 76.4 us -> 65.2 us
  waiting for transfers between devices: 25.4 us -> 15.8 us
    ppermute x1 -> x9, starting transfers between devices: 3.97 us -> 21.6 us  [the longest x7 14 us: body(): lax.ppermute(part, 'sec', [(i, i ^ away) for i in range(sections)])]
    all_to_all x1, blocking collectives: 34.5 us -> 23.2 us  [body(): high = lax.all_to_all(high, 'sec', split_axis=0, concat_axis=0, tiled=True)]
    ppermute x1 -> x9, waiting for transfers between devices: 25.4 us -> 15.8 us  [the longest x7 11 us: body(): lax.ppermute(part, 'sec', [(i, i ^ away) for i in range(sections)])]
    pallas_call x1 -> x2, Pallas kernels: 1.5 us -> 2.5 us  [warp(): pl.pallas_call(functools.partial(warp_kernel, first=first), in_specs=[pl....]
  transfers between devices with their start and end apart: 2 -> 10, of which waited for: 1 -> 5; matrix products, arithmetic and copies ran while one was open for 0% -> 0% of each run, Pallas kernels for 0% -> 1%
where the time goes in v6:
time: 111 us; the launch traced here: 110 us
  blocking collectives  65.2 us (59%)
  starting transfers between devices  21.9 us (20%)
  waiting for transfers between devices  15.8 us (14%)
  Pallas kernels  5.85 us (5%)
    all_to_all x1, blocking collectives, body(): lax.all_to_all(raw.reshape(rows, BLOCK, raw.shape[1]), 'row', split_axis=...  31.7 us
    all_to_all x1, blocking collectives, body(): high = lax.all_to_all(high, 'sec', split_axis=0, concat_axis=0, tiled=True)  23.2 us
    ppermute x7, starting transfers between devices, body(): lax.ppermute(part, 'sec', [(i, i ^ away) for i in range(sections)])  14 us
    ppermute x7, waiting for transfers between devices, body(): lax.ppermute(part, 'sec', [(i, i ^ away) for i in range(sections)])  11 us
    all_to_all x1, blocking collectives, body(): lax.all_to_all(result, 'sec', split_axis=0, concat_axis=0, tiled=True)  10.4 us
    ppermute x1, waiting for transfers between devices, body(): near = lax.ppermute(own[:, :FIRST], 'row', links)  4.81 us
    ppermute x1, starting transfers between devices, body(): far = lax.ppermute(own[:, FIRST:], 'row', links)  3.9 us
    ppermute x1, starting transfers between devices, body(): near = lax.ppermute(own[:, :FIRST], 'row', links)  3.77 us
  transfers between devices with their start and end apart: 10, of which 5 were waited for; matrix products, arithmetic and copies ran while one was open for 0% of the time, Pallas kernels for 1%

profile of v6, /device:TPU:25, one launch (start us, length us, event | category | flops | bytes accessed | tf_op | source)
XLA Modules:
  0.0 110.3 jit_solution(2788015250601281778)
XLA Ops:
  0.6 31.7 %all_to_all.15.own = bf16[16,128,512]{2,1,0:T(8,128)(2,1)S(1)} all-to-all(bf16[16,128,512]{2,1,0:T(8,128)(2,1)} %bitcast.18), channel_id=1, replica_groups=mesh['sec'=8,'row'=16] {'row'}, dimensions={0} | all-to-all | bytes 4194304 | tf_op jit(solution)/shard_map/all_to_all | solution.py:152
  32.3 0.2 collective-permute-start
  32.5 0.0 copy-start
  32.5 0.0 copy-start.1
  32.6 3.8 %collective-permute-start.1 = (bf16[16,32,512]{2,1,0:T(8,128)(2,1)S(1)}, bf16[16,32,512]{2,1,0:T(8,128)(2,1)S(1)}, u32[]{:S(2)}, u32[]{:S(2)}) collective-permute-start(bf16[16,32,512]{2,1,0:T(8,128)(2,1)S(1)} %slice.18), channel_id=1, source_target_pairs={{2,1},{4,3},{6,5},{8,7},{10,9},{12,11},{14,13},{1,2},{3,4},{5,6},{... | collective-permute-start | bytes 1572872 | tf_op jit(solution)/shard_map/ppermute | solution.py:159
  36.3 0.1 slice.19
  36.5 3.9 %collective-permute-start.9 = (bf16[16,96,512]{2,1,0:T(8,128)(2,1)S(1)}, bf16[16,96,512]{2,1,0:T(8,128)(2,1)S(1)}, u32[]{:S(2)}, u32[]{:S(2)}) collective-permute-start(bf16[16,96,512]{2,1,0:T(8,128)(2,1)S(1)} %slice.19), channel_id=1, source_target_pairs={{2,1},{4,3},{6,5},{8,7},{10,9},{12,11},{14,13},{1,2},{3,4},{5,6},{... | collective-permute-start | bytes 4718600 | tf_op jit(solution)/shard_map/ppermute | solution.py:160
  40.4 4.8 %collective-permute-done.1.across = bf16[16,32,512]{2,1,0:T(8,128)(2,1)S(1)} collective-permute-done((bf16[16,32,512]{2,1,0:T(8,128)(2,1)S(1)}, bf16[16,32,512]{2,1,0:T(8,128)(2,1)S(1)}, u32[]{:S(2)}, u32[]{:S(2)}) %collective-permute-start.1) | collective-permute-done | bytes 524320 | tf_op jit(solution)/shard_map/ppermute | solution.py:159
  45.2 0.0 collective-permute-done.beside
  45.2 0.0 copy-done
  45.2 0.0 copy-done.1
  45.2 1.1 warp.2
  46.3 1.7 %collective-permute-start.2 = (bf16[8,32,128]{2,1,0:T(8,128)(2,1)S(1)}, bf16[8,32,128]{2,1,0:T(8,128)(2,1)S(1)}, u32[]{:S(2)}, u32[]{:S(2)}) collective-permute-start(bf16[8,32,128]{2,1,0:T(8,128)(2,1)S(1)} %get-tuple-element.20), channel_id=1, source_target_pairs={{0,16},{16,0},{32,48},{48,32},{64,80},{80,64},{96,112},{112,96},{1... | collective-permute-start | bytes 196616 | tf_op jit(solution)/shard_map/ppermute | solution.py:165
  48.0 3.3 %collective-permute-start.3 = (bf16[8,32,128]{2,1,0:T(8,128)(2,1)S(1)}, bf16[8,32,128]{2,1,0:T(8,128)(2,1)S(1)}, u32[]{:S(2)}, u32[]{:S(2)}) collective-permute-start(bf16[8,32,128]{2,1,0:T(8,128)(2,1)S(1)} %get-tuple-element.21), channel_id=1, source_target_pairs={{0,32},{16,48},{32,0},{48,16},{64,96},{80,112},{96,64},{112,80},{1... | collective-permute-start | bytes 196616 | tf_op jit(solution)/shard_map/ppermute | solution.py:165
  51.3 0.0 collective-permute-start.4
  51.3 2.5 %collective-permute-start.5 = (bf16[8,32,128]{2,1,0:T(8,128)(2,1)S(1)}, bf16[8,32,128]{2,1,0:T(8,128)(2,1)S(1)}, u32[]{:S(2)}, u32[]{:S(2)}) collective-permute-start(bf16[8,32,128]{2,1,0:T(8,128)(2,1)S(1)} %get-tuple-element.23), channel_id=1, source_target_pairs={{0,64},{16,80},{32,96},{48,112},{64,0},{80,16},{96,32},{112,48},{1... | collective-permute-start | bytes 196616 | tf_op jit(solution)/shard_map/ppermute | solution.py:165
  53.8 0.0 collective-permute-done.2.refs_1_
  53.8 0.0 collective-permute-start.6
  53.8 0.0 collective-permute-done.3.refs_2_
  53.8 6.3 %collective-permute-start.7 = (bf16[8,32,128]{2,1,0:T(8,128)(2,1)S(1)}, bf16[8,32,128]{2,1,0:T(8,128)(2,1)S(1)}, u32[]{:S(2)}, u32[]{:S(2)}) collective-permute-start(bf16[8,32,128]{2,1,0:T(8,128)(2,1)S(1)} %get-tuple-element.25), channel_id=1, source_target_pairs={{0,96},{16,112},{32,64},{48,80},{64,32},{80,48},{96,0},{112,16},{1... | collective-permute-start | bytes 196616 | tf_op jit(solution)/shard_map/ppermute | solution.py:165
  60.0 0.0 collective-permute-done.4.refs_3_
  60.0 0.2 collective-permute-start.8
  60.3 5.4 %collective-permute-done.5.refs_4_ = bf16[8,32,128]{2,1,0:T(8,128)(2,1)S(1)} collective-permute-done((bf16[8,32,128]{2,1,0:T(8,128)(2,1)S(1)}, bf16[8,32,128]{2,1,0:T(8,128)(2,1)S(1)}, u32[]{:S(2)}, u32[]{:S(2)}) %collective-permute-start.5) | collective-permute-done | bytes 65568 | tf_op jit(solution)/shard_map/ppermute | solution.py:165
  65.7 2.4 %collective-permute-done.6.refs_5_ = bf16[8,32,128]{2,1,0:T(8,128)(2,1)S(1)} collective-permute-done((bf16[8,32,128]{2,1,0:T(8,128)(2,1)S(1)}, bf16[8,32,128]{2,1,0:T(8,128)(2,1)S(1)}, u32[]{:S(2)}, u32[]{:S(2)}) %collective-permute-start.6) | collective-permute-done | bytes 65568 | tf_op jit(solution)/shard_map/ppermute | solution.py:165
  68.0 2.4 %collective-permute-done.7.refs_6_ = bf16[8,32,128]{2,1,0:T(8,128)(2,1)S(1)} collective-permute-done((bf16[8,32,128]{2,1,0:T(8,128)(2,1)S(1)}, bf16[8,32,128]{2,1,0:T(8,128)(2,1)S(1)}, u32[]{:S(2)}, u32[]{:S(2)}) %collective-permute-start.7) | collective-permute-done | bytes 65568 | tf_op jit(solution)/shard_map/ppermute | solution.py:165
  70.4 0.9 collective-permute-done.8.refs_7_
  71.3 0.0 collective-permute-done.9.across
  71.3 1.4 %warp.3 = bf16[64,96,128]{2,1,0:T(8,128)(2,1)S(1)} custom-call(s32[64]{0:T(128)S(1)} %bitcast.15, s32[64]{0:T(128)S(1)} %bitcast.17, bf16[16,128,512]{2,1,0:T(8,128)(2,1)S(1)} %all_to_all.15.own, bf16[16,128,512]{2,1,0:T(8,128)(2,1)S(1)} %collective-permute-done.beside, bf16[16,96,512]{2,1,0:T(8,128)(2,1)S(1)} %collective-permute-done.9.across), custom_call_target="tpu_custom_call" | custom-call | bytes 6291456 | tf_op jit(solution)/shard_map/warp/pallas_call | solution.py:36
  72.7 23.2 %all_to_all.16.high = bf16[8,8,96,128]{3,2,1,0:T(8,128)(2,1)S(1)} all-to-all(bf16[8,8,96,128]{3,2,1,0:T(8,128)(2,1)S(1)} %bitcast.13), channel_id=1, replica_groups=mesh['sec'=8,'row'=16] {'sec'}, dimensions={0} | all-to-all | bytes 3145728 | tf_op jit(solution)/shard_map/all_to_all | solution.py:171
  95.9 3.4 %scores.1 = f32[8,2,3,8,128]{4,3,2,1,0:T(8,128)S(1)} custom-call(bf16[8,8,96,128]{3,2,1,0:T(8,128)(2,1)S(1)} %all_to_all.16.high, bf16[8,32,128]{2,1,0:T(8,128)(2,1)S(1)} %get-tuple-element.28.refs_0_, bf16[8,32,128]{2,1,0:T(8,128)(2,1)S(1)} %collective-permute-done.2.refs_1_, bf16[8,32,128]{2,1,0:T(8,128)(2,1)S(1)} %collective-permute-done.3.refs_2_, ...), custom_call_target="tpu_custom_call" | custom-call | flops 1207959552 | bytes 3145728 | tf_op jit(solution)/shard_map/scores/pallas_call | solution.py:129
  99.3 10.4 %all_to_all.17 = f32[8,2,3,8,128]{4,3,2,1,0:T(8,128)S(1)} all-to-all(f32[8,2,3,8,128]{4,3,2,1,0:T(8,128)S(1)} %scores.1), channel_id=1, replica_groups=mesh['sec'=8,'row'=16] {'sec'}, dimensions={0} | all-to-all | bytes 393216 | tf_op jit(solution)/shard_map/all_to_all | solution.py:173
  109.7 0.7 copy_bitcast_fusion
  (2 shorter events, 0.0 us)
Async XLA Ops:
  32.3 12.9 %collective-permute-start = (bf16[16,128,512]{2,1,0:T(8,128)(2,1)S(1)}, bf16[16,128,512]{2,1,0:T(8,128)(2,1)S(1)}, u32[]{:S(2)}, u32[]{:S(2)}) collective-permute-start(bf16[16,128,512]{2,1,0:T(8,128)(2,1)S(1)} %all_to_all.15.own), channel_id=1, source_target_pairs={{0,1},{1,0},{2,3},{3,2},{4,5},{5,4},{6,7},{7,6},{8,9},{9,8},{10,11... | collective-permute-start | bytes 6291464 | tf_op jit(solution)/shard_map/ppermute | solution.py:161
  32.5 12.6 %copy-start = (s32[1,1,64]{2,1,0:T(1,128)S(1)}, s32[1,1,64]{2,1,0:T(1,128)}, u32[]{:S(2)}) copy-start(s32[1,1,64]{2,1,0:T(1,128)} %param.4) | copy-start | bytes 772
  32.5 12.6 %copy-start.1 = (s32[1,1,64]{2,1,0:T(1,128)S(1)}, s32[1,1,64]{2,1,0:T(1,128)}, u32[]{:S(2)}) copy-start(s32[1,1,64]{2,1,0:T(1,128)} %param.5) | copy-start | bytes 772
  32.6 12.6 %collective-permute-start.1 = (bf16[16,32,512]{2,1,0:T(8,128)(2,1)S(1)}, bf16[16,32,512]{2,1,0:T(8,128)(2,1)S(1)}, u32[]{:S(2)}, u32[]{:S(2)}) collective-permute-start(bf16[16,32,512]{2,1,0:T(8,128)(2,1)S(1)} %slice.18), channel_id=1, source_target_pairs={{2,1},{4,3},{6,5},{8,7},{10,9},{12,11},{14,13},{1,2},{3,4},{5,6},{... | collective-permute-start | bytes 1572872 | tf_op jit(solution)/shard_map/ppermute | solution.py:159
  36.5 34.8 %collective-permute-start.9 = (bf16[16,96,512]{2,1,0:T(8,128)(2,1)S(1)}, bf16[16,96,512]{2,1,0:T(8,128)(2,1)S(1)}, u32[]{:S(2)}, u32[]{:S(2)}) collective-permute-start(bf16[16,96,512]{2,1,0:T(8,128)(2,1)S(1)} %slice.19), channel_id=1, source_target_pairs={{2,1},{4,3},{6,5},{8,7},{10,9},{12,11},{14,13},{1,2},{3,4},{5,6},{... | collective-permute-start | bytes 4718600 | tf_op jit(solution)/shard_map/ppermute | solution.py:160
  46.3 7.5 %collective-permute-start.2 = (bf16[8,32,128]{2,1,0:T(8,128)(2,1)S(1)}, bf16[8,32,128]{2,1,0:T(8,128)(2,1)S(1)}, u32[]{:S(2)}, u32[]{:S(2)}) collective-permute-start(bf16[8,32,128]{2,1,0:T(8,128)(2,1)S(1)} %get-tuple-element.20), channel_id=1, source_target_pairs={{0,16},{16,0},{32,48},{48,32},{64,80},{80,64},{96,112},{112,96},{1... | collective-permute-start | bytes 196616 | tf_op jit(solution)/shard_map/ppermute | solution.py:165
  48.0 5.8 %collective-permute-start.3 = (bf16[8,32,128]{2,1,0:T(8,128)(2,1)S(1)}, bf16[8,32,128]{2,1,0:T(8,128)(2,1)S(1)}, u32[]{:S(2)}, u32[]{:S(2)}) collective-permute-start(bf16[8,32,128]{2,1,0:T(8,128)(2,1)S(1)} %get-tuple-element.21), channel_id=1, source_target_pairs={{0,32},{16,48},{32,0},{48,16},{64,96},{80,112},{96,64},{112,80},{1... | collective-permute-start | bytes 196616 | tf_op jit(solution)/shard_map/ppermute | solution.py:165
  51.3 8.7 %collective-permute-start.4 = (bf16[8,32,128]{2,1,0:T(8,128)(2,1)S(1)}, bf16[8,32,128]{2,1,0:T(8,128)(2,1)S(1)}, u32[]{:S(2)}, u32[]{:S(2)}) collective-permute-start(bf16[8,32,128]{2,1,0:T(8,128)(2,1)S(1)} %get-tuple-element.22), channel_id=1, source_target_pairs={{0,48},{16,32},{32,16},{48,0},{64,112},{80,96},{96,80},{112,64},{1... | collective-permute-start | bytes 196616 | tf_op jit(solution)/shard_map/ppermute | solution.py:165
  51.3 14.4 %collective-permute-start.5 = (bf16[8,32,128]{2,1,0:T(8,128)(2,1)S(1)}, bf16[8,32,128]{2,1,0:T(8,128)(2,1)S(1)}, u32[]{:S(2)}, u32[]{:S(2)}) collective-permute-start(bf16[8,32,128]{2,1,0:T(8,128)(2,1)S(1)} %get-tuple-element.23), channel_id=1, source_target_pairs={{0,64},{16,80},{32,96},{48,112},{64,0},{80,16},{96,32},{112,48},{1... | collective-permute-start | bytes 196616 | tf_op jit(solution)/shard_map/ppermute | solution.py:165
  53.8 14.3 %collective-permute-start.6 = (bf16[8,32,128]{2,1,0:T(8,128)(2,1)S(1)}, bf16[8,32,128]{2,1,0:T(8,128)(2,1)S(1)}, u32[]{:S(2)}, u32[]{:S(2)}) collective-permute-start(bf16[8,32,128]{2,1,0:T(8,128)(2,1)S(1)} %get-tuple-element.24), channel_id=1, source_target_pairs={{0,80},{16,64},{32,112},{48,96},{64,16},{80,0},{96,48},{112,32},{1... | collective-permute-start | bytes 196616 | tf_op jit(solution)/shard_map/ppermute | solution.py:165
  53.8 16.6 %collective-permute-start.7 = (bf16[8,32,128]{2,1,0:T(8,128)(2,1)S(1)}, bf16[8,32,128]{2,1,0:T(8,128)(2,1)S(1)}, u32[]{:S(2)}, u32[]{:S(2)}) collective-permute-start(bf16[8,32,128]{2,1,0:T(8,128)(2,1)S(1)} %get-tuple-element.25), channel_id=1, source_target_pairs={{0,96},{16,112},{32,64},{48,80},{64,32},{80,48},{96,0},{112,16},{1... | collective-permute-start | bytes 196616 | tf_op jit(solution)/shard_map/ppermute | solution.py:165
  60.0 11.2 %collective-permute-start.8 = (bf16[8,32,128]{2,1,0:T(8,128)(2,1)S(1)}, bf16[8,32,128]{2,1,0:T(8,128)(2,1)S(1)}, u32[]{:S(2)}, u32[]{:S(2)}) collective-permute-start(bf16[8,32,128]{2,1,0:T(8,128)(2,1)S(1)} %get-tuple-element.26), channel_id=1, source_target_pairs={{0,112},{16,96},{32,80},{48,64},{64,48},{80,32},{96,16},{112,0},{1... | collective-permute-start | bytes 196616 | tf_op jit(solution)/shard_map/ppermute | solution.py:165

commit v7 on v6

--- a/solution.py
+++ b/solution.py
@@ -9,7 +9,7 @@
 
 BLOCK = 128
 LAGS = 3
-FIRST = 32
+FIRST = 16
 
 
 def warp_kernel(shifts, columns, own, beside, across, *outs, first):
@@ -160,7 +160,7 @@
     far = lax.ppermute(own[:, FIRST:], "row", links)
     beside = lax.ppermute(own, "row", [(i, i ^ 1) for i in range(rows)])
 
-    lows = warp(shifts, columns, own, beside, near, 0, sections, 12000000000)
+    lows = warp(shifts, columns, own, beside, near, 0, sections, 60000000000)
     lows = [
         part if away == 0 else lax.ppermute(part, "sec", [(i, i ^ away) for i in range(sections)])
         for away, part in enumerate(lows)

time: 111 us -> 110 us (level)
  waiting for transfers between devices: 15.8 us -> 14.2 us
    ppermute x1, waiting for transfers between devices: 4.81 us -> 1.94 us  [body(): near = lax.ppermute(own[:, :FIRST], 'row', links)]
    ppermute x7, waiting for transfers between devices: 11 us -> 12.3 us  [body(): lax.ppermute(part, 'sec', [(i, i ^ away) for i in range(sections)])]
where the time goes in v7:
time: 110 us; the launch traced here: 109 us
  blocking collectives  65.4 us (59%)
  starting transfers between devices  21.9 us (20%)
  waiting for transfers between devices  14.2 us (13%)
  Pallas kernels  5.9 us (5%)
    all_to_all x1, blocking collectives, body(): lax.all_to_all(raw.reshape(rows, BLOCK, raw.shape[1]), 'row', split_axis=...  31.7 us
    all_to_all x1, blocking collectives, body(): high = lax.all_to_all(high, 'sec', split_axis=0, concat_axis=0, tiled=True)  24 us
    ppermute x7, starting transfers between devices, body(): lax.ppermute(part, 'sec', [(i, i ^ away) for i in range(sections)])  14 us
    ppermute x7, waiting for transfers between devices, body(): lax.ppermute(part, 'sec', [(i, i ^ away) for i in range(sections)])  12.3 us
    all_to_all x1, blocking collectives, body(): lax.all_to_all(result, 'sec', split_axis=0, concat_axis=0, tiled=True)  9.69 us
    ppermute x1, starting transfers between devices, body(): far = lax.ppermute(own[:, FIRST:], 'row', links)  3.9 us
    ppermute x1, starting transfers between devices, body(): near = lax.ppermute(own[:, :FIRST], 'row', links)  3.77 us
    pallas_call x1, Pallas kernels, scores(): pl.pallas_call(score_kernel, in_specs=[pl.BlockSpec(memory_space=pltpu.VM...  3.35 us
  transfers between devices with their start and end apart: 10, of which 5 were waited for; matrix products, arithmetic and copies ran while one was open for 0% of the time, Pallas kernels for 1%

profile of v7, /device:TPU:25, one launch (start us, length us, event | category | flops | bytes accessed | tf_op | source)
XLA Modules:
  0.0 109.0 jit_solution(10262256880789246380)
XLA Ops:
  0.6 31.7 %all_to_all.15.own = bf16[16,128,512]{2,1,0:T(8,128)(2,1)S(1)} all-to-all(bf16[16,128,512]{2,1,0:T(8,128)(2,1)} %bitcast.18), channel_id=1, replica_groups=mesh['sec'=8,'row'=16] {'row'}, dimensions={0} | all-to-all | bytes 4194304 | tf_op jit(solution)/shard_map/all_to_all | solution.py:152
  32.3 0.2 collective-permute-start
  32.5 0.0 copy-start
  32.5 0.0 copy-start.1
  32.5 3.8 %collective-permute-start.1 = (bf16[16,16,512]{2,1,0:T(8,128)(2,1)S(1)}, bf16[16,16,512]{2,1,0:T(8,128)(2,1)S(1)}, u32[]{:S(2)}, u32[]{:S(2)}) collective-permute-start(bf16[16,16,512]{2,1,0:T(8,128)(2,1)S(1)} %slice.18), channel_id=1, source_target_pairs={{2,1},{4,3},{6,5},{8,7},{10,9},{12,11},{14,13},{1,2},{3,4},{5,6},{... | collective-permute-start | bytes 786440 | tf_op jit(solution)/shard_map/ppermute | solution.py:159
  36.3 0.2 slice.19
  36.5 3.9 %collective-permute-start.9 = (bf16[16,112,512]{2,1,0:T(8,128)(2,1)S(1)}, bf16[16,112,512]{2,1,0:T(8,128)(2,1)S(1)}, u32[]{:S(2)}, u32[]{:S(2)}) collective-permute-start(bf16[16,112,512]{2,1,0:T(8,128)(2,1)S(1)} %slice.19), channel_id=1, source_target_pairs={{2,1},{4,3},{6,5},{8,7},{10,9},{12,11},{14,13},{1,2},{3,4},{5,6},{... | collective-permute-start | bytes 5505032 | tf_op jit(solution)/shard_map/ppermute | solution.py:160
  40.4 1.9 %collective-permute-done.1.across = bf16[16,16,512]{2,1,0:T(8,128)(2,1)S(1)} collective-permute-done((bf16[16,16,512]{2,1,0:T(8,128)(2,1)S(1)}, bf16[16,16,512]{2,1,0:T(8,128)(2,1)S(1)}, u32[]{:S(2)}, u32[]{:S(2)}) %collective-permute-start.1) | collective-permute-done | bytes 262176 | tf_op jit(solution)/shard_map/ppermute | solution.py:159
  42.3 0.0 collective-permute-done.beside
  42.4 0.0 copy-done
  42.4 0.0 copy-done.1
  42.4 1.1 warp.2
  43.4 1.7 %collective-permute-start.2 = (bf16[8,16,128]{2,1,0:T(8,128)(2,1)S(1)}, bf16[8,16,128]{2,1,0:T(8,128)(2,1)S(1)}, u32[]{:S(2)}, u32[]{:S(2)}) collective-permute-start(bf16[8,16,128]{2,1,0:T(8,128)(2,1)S(1)} %get-tuple-element.20), channel_id=1, source_target_pairs={{0,16},{16,0},{32,48},{48,32},{64,80},{80,64},{96,112},{112,96},{1... | collective-permute-start | bytes 98312 | tf_op jit(solution)/shard_map/ppermute | solution.py:165
  45.2 3.3 %collective-permute-start.3 = (bf16[8,16,128]{2,1,0:T(8,128)(2,1)S(1)}, bf16[8,16,128]{2,1,0:T(8,128)(2,1)S(1)}, u32[]{:S(2)}, u32[]{:S(2)}) collective-permute-start(bf16[8,16,128]{2,1,0:T(8,128)(2,1)S(1)} %get-tuple-element.21), channel_id=1, source_target_pairs={{0,32},{16,48},{32,0},{48,16},{64,96},{80,112},{96,64},{112,80},{1... | collective-permute-start | bytes 98312 | tf_op jit(solution)/shard_map/ppermute | solution.py:165
  48.5 0.0 collective-permute-start.4
  48.5 2.5 %collective-permute-start.5 = (bf16[8,16,128]{2,1,0:T(8,128)(2,1)S(1)}, bf16[8,16,128]{2,1,0:T(8,128)(2,1)S(1)}, u32[]{:S(2)}, u32[]{:S(2)}) collective-permute-start(bf16[8,16,128]{2,1,0:T(8,128)(2,1)S(1)} %get-tuple-element.23), channel_id=1, source_target_pairs={{0,64},{16,80},{32,96},{48,112},{64,0},{80,16},{96,32},{112,48},{1... | collective-permute-start | bytes 98312 | tf_op jit(solution)/shard_map/ppermute | solution.py:165
  50.9 0.0 collective-permute-done.2.refs_1_
  50.9 0.0 collective-permute-start.6
  50.9 0.0 collective-permute-done.3.refs_2_
  50.9 6.3 %collective-permute-start.7 = (bf16[8,16,128]{2,1,0:T(8,128)(2,1)S(1)}, bf16[8,16,128]{2,1,0:T(8,128)(2,1)S(1)}, u32[]{:S(2)}, u32[]{:S(2)}) collective-permute-start(bf16[8,16,128]{2,1,0:T(8,128)(2,1)S(1)} %get-tuple-element.25), channel_id=1, source_target_pairs={{0,96},{16,112},{32,64},{48,80},{64,32},{80,48},{96,0},{112,16},{1... | collective-permute-start | bytes 98312 | tf_op jit(solution)/shard_map/ppermute | solution.py:165
  57.2 0.0 collective-permute-done.4.refs_3_
  57.2 0.2 collective-permute-start.8
  57.4 7.8 %collective-permute-done.5.refs_4_ = bf16[8,16,128]{2,1,0:T(8,128)(2,1)S(1)} collective-permute-done((bf16[8,16,128]{2,1,0:T(8,128)(2,1)S(1)}, bf16[8,16,128]{2,1,0:T(8,128)(2,1)S(1)}, u32[]{:S(2)}, u32[]{:S(2)}) %collective-permute-start.5) | collective-permute-done | bytes 32800 | tf_op jit(solution)/shard_map/ppermute | solution.py:165
  65.2 1.7 %collective-permute-done.6.refs_5_ = bf16[8,16,128]{2,1,0:T(8,128)(2,1)S(1)} collective-permute-done((bf16[8,16,128]{2,1,0:T(8,128)(2,1)S(1)}, bf16[8,16,128]{2,1,0:T(8,128)(2,1)S(1)}, u32[]{:S(2)}, u32[]{:S(2)}) %collective-permute-start.6) | collective-permute-done | bytes 32800 | tf_op jit(solution)/shard_map/ppermute | solution.py:165
  66.9 2.3 %collective-permute-done.7.refs_6_ = bf16[8,16,128]{2,1,0:T(8,128)(2,1)S(1)} collective-permute-done((bf16[8,16,128]{2,1,0:T(8,128)(2,1)S(1)}, bf16[8,16,128]{2,1,0:T(8,128)(2,1)S(1)}, u32[]{:S(2)}, u32[]{:S(2)}) %collective-permute-start.7) | collective-permute-done | bytes 32800 | tf_op jit(solution)/shard_map/ppermute | solution.py:165
  69.2 0.5 collective-permute-done.8.refs_7_
  69.7 0.0 collective-permute-done.9.across
  69.7 1.5 %warp.3 = bf16[64,112,128]{2,1,0:T(8,128)(2,1)S(1)} custom-call(s32[64]{0:T(128)S(1)} %bitcast.15, s32[64]{0:T(128)S(1)} %bitcast.17, bf16[16,128,512]{2,1,0:T(8,128)(2,1)S(1)} %all_to_all.15.own, bf16[16,128,512]{2,1,0:T(8,128)(2,1)S(1)} %collective-permute-done.beside, bf16[16,112,512]{2,1,0:T(8,128)(2,1)S(1)} %collective-permute-done.9.across), custom_call_target="tpu_custom_call" | custom-call | bytes 7340032 | tf_op jit(solution)/shard_map/warp/pallas_call | solution.py:36
  71.2 24.0 %all_to_all.16.high = bf16[8,8,112,128]{3,2,1,0:T(8,128)(2,1)S(1)} all-to-all(bf16[8,8,112,128]{3,2,1,0:T(8,128)(2,1)S(1)} %bitcast.13), channel_id=1, replica_groups=mesh['sec'=8,'row'=16] {'sec'}, dimensions={0} | all-to-all | bytes 3670016 | tf_op jit(solution)/shard_map/all_to_all | solution.py:171
  95.2 3.3 %scores.1 = f32[8,2,3,8,128]{4,3,2,1,0:T(8,128)S(1)} custom-call(bf16[8,8,112,128]{3,2,1,0:T(8,128)(2,1)S(1)} %all_to_all.16.high, bf16[8,16,128]{2,1,0:T(8,128)(2,1)S(1)} %get-tuple-element.28.refs_0_, bf16[8,16,128]{2,1,0:T(8,128)(2,1)S(1)} %collective-permute-done.2.refs_1_, bf16[8,16,128]{2,1,0:T(8,128)(2,1)S(1)} %collective-permute-done.3.refs_2_, ...), custom_call_target="tpu_custom_call" | custom-call | flops 1207959552 | bytes 3670016 | tf_op jit(solution)/shard_map/scores/pallas_call | solution.py:129
  98.6 9.7 %all_to_all.17 = f32[8,2,3,8,128]{4,3,2,1,0:T(8,128)S(1)} all-to-all(f32[8,2,3,8,128]{4,3,2,1,0:T(8,128)S(1)} %scores.1), channel_id=1, replica_groups=mesh['sec'=8,'row'=16] {'sec'}, dimensions={0} | all-to-all | bytes 393216 | tf_op jit(solution)/shard_map/all_to_all | solution.py:173
  108.3 0.7 copy_bitcast_fusion
  (2 shorter events, 0.0 us)
Async XLA Ops:
  32.3 10.1 %collective-permute-start = (bf16[16,128,512]{2,1,0:T(8,128)(2,1)S(1)}, bf16[16,128,512]{2,1,0:T(8,128)(2,1)S(1)}, u32[]{:S(2)}, u32[]{:S(2)}) collective-permute-start(bf16[16,128,512]{2,1,0:T(8,128)(2,1)S(1)} %all_to_all.15.own), channel_id=1, source_target_pairs={{0,1},{1,0},{2,3},{3,2},{4,5},{5,4},{6,7},{7,6},{8,9},{9,8},{10,11... | collective-permute-start | bytes 6291464 | tf_op jit(solution)/shard_map/ppermute | solution.py:161
  32.5 9.8 %copy-start = (s32[1,1,64]{2,1,0:T(1,128)S(1)}, s32[1,1,64]{2,1,0:T(1,128)}, u32[]{:S(2)}) copy-start(s32[1,1,64]{2,1,0:T(1,128)} %param.4) | copy-start | bytes 772
  32.5 9.8 %copy-start.1 = (s32[1,1,64]{2,1,0:T(1,128)S(1)}, s32[1,1,64]{2,1,0:T(1,128)}, u32[]{:S(2)}) copy-start(s32[1,1,64]{2,1,0:T(1,128)} %param.5) | copy-start | bytes 772
  32.5 9.8 %collective-permute-start.1 = (bf16[16,16,512]{2,1,0:T(8,128)(2,1)S(1)}, bf16[16,16,512]{2,1,0:T(8,128)(2,1)S(1)}, u32[]{:S(2)}, u32[]{:S(2)}) collective-permute-start(bf16[16,16,512]{2,1,0:T(8,128)(2,1)S(1)} %slice.18), channel_id=1, source_target_pairs={{2,1},{4,3},{6,5},{8,7},{10,9},{12,11},{14,13},{1,2},{3,4},{5,6},{... | collective-permute-start | bytes 786440 | tf_op jit(solution)/shard_map/ppermute | solution.py:159
  36.5 33.2 %collective-permute-start.9 = (bf16[16,112,512]{2,1,0:T(8,128)(2,1)S(1)}, bf16[16,112,512]{2,1,0:T(8,128)(2,1)S(1)}, u32[]{:S(2)}, u32[]{:S(2)}) collective-permute-start(bf16[16,112,512]{2,1,0:T(8,128)(2,1)S(1)} %slice.19), channel_id=1, source_target_pairs={{2,1},{4,3},{6,5},{8,7},{10,9},{12,11},{14,13},{1,2},{3,4},{5,6},{... | collective-permute-start | bytes 5505032 | tf_op jit(solution)/shard_map/ppermute | solution.py:160
  43.4 7.5 %collective-permute-start.2 = (bf16[8,16,128]{2,1,0:T(8,128)(2,1)S(1)}, bf16[8,16,128]{2,1,0:T(8,128)(2,1)S(1)}, u32[]{:S(2)}, u32[]{:S(2)}) collective-permute-start(bf16[8,16,128]{2,1,0:T(8,128)(2,1)S(1)} %get-tuple-element.20), channel_id=1, source_target_pairs={{0,16},{16,0},{32,48},{48,32},{64,80},{80,64},{96,112},{112,96},{1... | collective-permute-start | bytes 98312 | tf_op jit(solution)/shard_map/ppermute | solution.py:165
  45.2 5.8 %collective-permute-start.3 = (bf16[8,16,128]{2,1,0:T(8,128)(2,1)S(1)}, bf16[8,16,128]{2,1,0:T(8,128)(2,1)S(1)}, u32[]{:S(2)}, u32[]{:S(2)}) collective-permute-start(bf16[8,16,128]{2,1,0:T(8,128)(2,1)S(1)} %get-tuple-element.21), channel_id=1, source_target_pairs={{0,32},{16,48},{32,0},{48,16},{64,96},{80,112},{96,64},{112,80},{1... | collective-permute-start | bytes 98312 | tf_op jit(solution)/shard_map/ppermute | solution.py:165
  48.5 8.7 %collective-permute-start.4 = (bf16[8,16,128]{2,1,0:T(8,128)(2,1)S(1)}, bf16[8,16,128]{2,1,0:T(8,128)(2,1)S(1)}, u32[]{:S(2)}, u32[]{:S(2)}) collective-permute-start(bf16[8,16,128]{2,1,0:T(8,128)(2,1)S(1)} %get-tuple-element.22), channel_id=1, source_target_pairs={{0,48},{16,32},{32,16},{48,0},{64,112},{80,96},{96,80},{112,64},{1... | collective-permute-start | bytes 98312 | tf_op jit(solution)/shard_map/ppermute | solution.py:165
  48.5 16.7 %collective-permute-start.5 = (bf16[8,16,128]{2,1,0:T(8,128)(2,1)S(1)}, bf16[8,16,128]{2,1,0:T(8,128)(2,1)S(1)}, u32[]{:S(2)}, u32[]{:S(2)}) collective-permute-start(bf16[8,16,128]{2,1,0:T(8,128)(2,1)S(1)} %get-tuple-element.23), channel_id=1, source_target_pairs={{0,64},{16,80},{32,96},{48,112},{64,0},{80,16},{96,32},{112,48},{1... | collective-permute-start | bytes 98312 | tf_op jit(solution)/shard_map/ppermute | solution.py:165
  50.9 16.0 %collective-permute-start.6 = (bf16[8,16,128]{2,1,0:T(8,128)(2,1)S(1)}, bf16[8,16,128]{2,1,0:T(8,128)(2,1)S(1)}, u32[]{:S(2)}, u32[]{:S(2)}) collective-permute-start(bf16[8,16,128]{2,1,0:T(8,128)(2,1)S(1)} %get-tuple-element.24), channel_id=1, source_target_pairs={{0,80},{16,64},{32,112},{48,96},{64,16},{80,0},{96,48},{112,32},{1... | collective-permute-start | bytes 98312 | tf_op jit(solution)/shard_map/ppermute | solution.py:165
  50.9 18.3 %collective-permute-start.7 = (bf16[8,16,128]{2,1,0:T(8,128)(2,1)S(1)}, bf16[8,16,128]{2,1,0:T(8,128)(2,1)S(1)}, u32[]{:S(2)}, u32[]{:S(2)}) collective-permute-start(bf16[8,16,128]{2,1,0:T(8,128)(2,1)S(1)} %get-tuple-element.25), channel_id=1, source_target_pairs={{0,96},{16,112},{32,64},{48,80},{64,32},{80,48},{96,0},{112,16},{1... | collective-permute-start | bytes 98312 | tf_op jit(solution)/shard_map/ppermute | solution.py:165
  57.2 12.5 %collective-permute-start.8 = (bf16[8,16,128]{2,1,0:T(8,128)(2,1)S(1)}, bf16[8,16,128]{2,1,0:T(8,128)(2,1)S(1)}, u32[]{:S(2)}, u32[]{:S(2)}) collective-permute-start(bf16[8,16,128]{2,1,0:T(8,128)(2,1)S(1)} %get-tuple-element.26), channel_id=1, source_target_pairs={{0,112},{16,96},{32,80},{48,64},{64,48},{80,32},{96,16},{112,0},{1... | collective-permute-start | bytes 98312 | tf_op jit(solution)/shard_map/ppermute | solution.py:165
